TPU v7x, 256 devices: a whole 4x4x8 slice. The times are simulated.
256 devices in a mesh: section: 8 (over y, core), expert: 32 (over z, x).
Axes of the slice: x: 4, y: 4, z: 8, core: 2. Of those that a mesh axis runs over, the one named last changes fastest.
Arguments:
- tokens_ahead: bfloat16 [8, 512, 3584], P('section', 'expert'), may hold values from -6 to 6
- tokens_behind: bfloat16 [8, 512, 3584], P('section', 'expert'), may hold values from -6 to 6
- routes_ahead: int32 [1, 8, 512, 8], P(None, None, 'expert'), may hold values from 0 to 31, all different within a row; in each aligned block of 16 rows (0 to 15, 16 to 31, ..., all dimensions but the last counted through in order) at most 5 rows name the same one
- routes_behind: int32 [1, 8, 512, 8], P(None, None, 'expert'), may hold values from 0 to 31, all different within a row; in each aligned block of 16 rows (0 to 15, 16 to 31, ..., all dimensions but the last counted through in order) at most 5 rows name the same one
- gates_ahead: float32 [1, 8, 512, 8], P(None, None, 'expert'), may hold values from 0.1 to 1
- gates_behind: float32 [1, 8, 512, 8], P(None, None, 'expert'), may hold values from 0.1 to 1
- gate_proj: bfloat16 [8, 32, 3584, 512], P('section', 'expert'), may hold values from -0.09375 to 0.09375
- up_proj: bfloat16 [8, 32, 3584, 512], P('section', 'expert'), may hold values from -0.09375 to 0.09375
- down_proj: bfloat16 [8, 32, 512, 3584], P('section', 'expert'), may hold values from -0.1875 to 0.1875
Outputs:
- ahead_states: bfloat16 [8, 512, 3584], P('section', 'expert')
- behind_states: bfloat16 [8, 512, 3584], P('section', 'expert')
Inputs may be any that keep to these rules, and one draw needn't show every extreme that they name: `routes_ahead`: in each aligned block of 16 tokens (the tokens of one device) no expert is named by more than 5 routes, a bound that some block reaches; a token names 8 different experts. `routes_behind`: in each aligned block of 16 tokens no expert is named by more than 5 routes, a bound that some block reaches; a token names 8 different experts.
All inputs are finite; a program needn't handle non-finite values.
Results may differ from a plain program's by a relative error of at most 0.01.
Values may be sent and summed in bfloat16 or wider, within the bound.
A program may use at most 128 MiB of HBM per device.

v0:
```python
import jax
import jax.numpy as jnp
from jax import lax
from jax.sharding import PartitionSpec as P


def swapped(block, axis, stride):
    count = lax.axis_size(axis)
    route = []
    for low in range(count):
        high = low | 1 << stride
        if high != low and high < count:
            route += [(low, high), (high, low)]
    return lax.ppermute(block, axis, route)


def passed_along(value, axis, steps):
    count = lax.axis_size(axis)
    pairs = [(source, (source + steps) % count) for source in range(count)]
    return lax.ppermute(value, axis, pairs)


def normalize(buffer):
    values = buffer.astype(jnp.float32)
    scale_row = lax.rsqrt(jnp.mean(values * values, axis=-1, keepdims=True) + 1e-06)
    return (values * scale_row).astype(jnp.bfloat16)


def slot_index(ids, experts_n, capacity):
    flat_ids = ids.reshape(-1)
    onehot = (flat_ids[:, None] == jnp.arange(experts_n, dtype=jnp.int32)[None, :]).astype(
        jnp.int32
    )
    before = jnp.cumsum(onehot, axis=0) - onehot
    position = jnp.sum(before * onehot, axis=1)
    return flat_ids * capacity + position


def dispatch_matrix(slot_ids, row_count, top_count, slot_total):
    matches = (
        slot_ids.reshape(row_count, top_count)[None, :, :]
        == jnp.arange(slot_total, dtype=jnp.int32)[:, None, None]
    )
    return jnp.any(matches, axis=2).astype(jnp.bfloat16)


def expert(arrived, gate_local, up_local, down_local):
    gate_out = jnp.dot(arrived, gate_local, preferred_element_type=jnp.float32)
    up_out = jnp.dot(arrived, up_local, preferred_element_type=jnp.float32)
    hidden = (jax.nn.silu(gate_out) * up_out).astype(jnp.bfloat16)
    return jnp.dot(hidden, down_local, preferred_element_type=jnp.float32).astype(jnp.bfloat16)


def mixing(slot_ids, gate_weights, returned):
    row_count, top_count = gate_weights.shape
    picked = (
        jnp.take(returned, slot_ids, axis=0).reshape(row_count, top_count, -1).astype(jnp.float32)
    )
    return jnp.einsum("rk,rkd->rd", gate_weights, picked)


def capacity_of(row_count, top_count, experts_n):
    spread = row_count * top_count
    return min(row_count, max(2, spread // experts_n + spread // (4 * experts_n)))


def prepare(normed, ids, experts_n, capacity):
    row_count, top_count = ids.shape
    slot_ids = slot_index(ids, experts_n, capacity)
    matrix = dispatch_matrix(slot_ids, row_count, top_count, experts_n * capacity)
    outgoing = jnp.dot(matrix, normed, preferred_element_type=jnp.float32).astype(jnp.bfloat16)
    return (outgoing.reshape(experts_n, capacity, normed.shape[-1]), slot_ids)


def partner_rows(normed):
    return swapped(normed, "section", 0)


def partner_mix(mixed):
    return swapped(mixed.astype(jnp.bfloat16), "section", 0).astype(mixed.dtype)


def body(
    tokens_ahead,
    tokens_behind,
    routes_ahead,
    routes_behind,
    gates_ahead,
    gates_behind,
    gate_proj,
    up_proj,
    down_proj,
):
    experts_n = lax.axis_size("expert")
    section_at = lax.axis_index("section")
    partner_at = section_at + 1 - 2 * (section_at % 2)
    gate_local = gate_proj[0, 0]
    up_local = up_proj[0, 0]
    down_local = down_proj[0, 0]
    ahead_state = tokens_ahead[0]
    behind_state = tokens_behind[0]
    row_count = ahead_state.shape[0]
    width = ahead_state.shape[1]
    top_count = routes_ahead.shape[-1]
    capacity = capacity_of(row_count, top_count, experts_n)

    def select(table, turn_index, where):
        return lax.dynamic_index_in_dim(table[turn_index], where, 0, keepdims=False)

    def compute(arrived):
        flat_rows = arrived.reshape(-1, width)
        return expert(flat_rows, gate_local, up_local, down_local).reshape(arrived.shape)

    def begin(state, ids_own, ids_other):
        normed = normalize(state)
        other_rows = partner_rows(normed)
        out_own, slots_own = prepare(normed, ids_own, experts_n, capacity)
        out_other, slots_other = prepare(other_rows, ids_other, experts_n, capacity)
        return (jnp.concatenate([out_own, out_other], axis=1), slots_own, slots_other)

    def finish(state, returned, slots_own, slots_other, weights_own, weights_other):
        own_mix = mixing(slots_own, weights_own, returned[:, :capacity].reshape(-1, width))
        other_mix = mixing(slots_other, weights_other, returned[:, capacity:].reshape(-1, width))
        total = state.astype(jnp.float32) + own_mix + partner_mix(other_mix)
        return total.astype(jnp.bfloat16)

    def apart_pass(state, ids_own, ids_other, weights_own, weights_other):
        outgoing, slots_own, slots_other = begin(state, ids_own, ids_other)
        returned = lax.all_to_all(
            compute(lax.all_to_all(outgoing, "expert", split_axis=0, concat_axis=0, tiled=True)),
            "expert",
            split_axis=0,
            concat_axis=0,
            tiled=True,
        )
        return finish(state, returned, slots_own, slots_other, weights_own, weights_other)

    turn_index = 0
    ahead_state = passed_along(ahead_state, "section", 2)
    behind_state = passed_along(behind_state, "section", -2)
    ids_ahead = select(routes_ahead, turn_index, section_at)
    ids_ahead_other = select(routes_ahead, turn_index, partner_at)
    ids_behind = select(routes_behind, turn_index, section_at)
    ids_behind_other = select(routes_behind, turn_index, partner_at)
    weights_ahead = select(gates_ahead, turn_index, section_at)
    weights_ahead_other = select(gates_ahead, turn_index, partner_at)
    weights_behind = select(gates_behind, turn_index, section_at)
    weights_behind_other = select(gates_behind, turn_index, partner_at)
    ahead_state = apart_pass(
        ahead_state, ids_ahead, ids_ahead_other, weights_ahead, weights_ahead_other
    )
    behind_state = apart_pass(
        behind_state, ids_behind, ids_behind_other, weights_behind, weights_behind_other
    )
    return (ahead_state[None], behind_state[None])


def solution(mesh):
    in_specs = (
        P("section", "expert", None),
        P("section", "expert", None),
        P(None, None, "expert", None),
        P(None, None, "expert", None),
        P(None, None, "expert", None),
        P(None, None, "expert", None),
        P("section", "expert", None, None),
        P("section", "expert", None, None),
        P("section", "expert", None, None),
    )
    out_specs = (P("section", "expert", None), P("section", "expert", None))
    return jax.shard_map(body, mesh=mesh, in_specs=in_specs, out_specs=out_specs, check_vma=False)
```

profile of v0, /device:TPU:4, one launch (start us, length us, event | category | flops | bytes accessed | tf_op | source)
XLA Modules:
  0.0 399.1 jit_solution(6906438127809883189)
XLA Ops:
  0.6 3.1 collective-permute-start.3
  8.6 1.5 reshape.162
  10.1 4.6 %pad_maximum_fusion.1 = bf16[32,10,3584]{2,1,0:T(8,128)(2,1)} fusion(bf16[32,5,3584]{2,1,0:T(8,128)(2,1)} %reshape.162, bf16[32,5,3584]{2,1,0:T(8,128)(2,1)S(1)} %reshape.161), kind=kLoop, calls=%fused_computation.11 | loop fusion | flops 4587520 | bytes 4587520 | tf_op jit(solution)/shard_map/concatenate | solution.py:119
  14.7 11.8 %all-to-all-start.2 = ((bf16[32,10,3584]{2,1,0:T(8,128)(2,1)}), bf16[32,10,3584]{2,1,0:T(8,128)(2,1)}, u32[]{:S(2)}, u32[]{:S(2)}) async-start(bf16[32,10,3584]{2,1,0:T(8,128)(2,1)} %pad_maximum_fusion.1), calls=%async_computation.2 | async-start | bytes 7340032 | tf_op jit(solution)/shard_map/all_to_all | solution.py:130
  30.1 2.9 collective-permute-done
  36.7 4.5 %pad_maximum_fusion = bf16[32,10,3584]{2,1,0:T(8,128)(2,1)} fusion(bf16[32,5,3584]{2,1,0:T(8,128)(2,1)} %reshape.154, bf16[32,5,3584]{2,1,0:T(8,128)(2,1)S(1)} %reshape.153), kind=kLoop, calls=%fused_computation.10 | loop fusion | flops 4587520 | bytes 4587520 | tf_op jit(solution)/shard_map/concatenate | solution.py:119
  41.2 67.5 %all-to-all-done.2 = bf16[32,10,3584]{2,1,0:T(8,128)(2,1)} async-done(((bf16[32,10,3584]{2,1,0:T(8,128)(2,1)}), bf16[32,10,3584]{2,1,0:T(8,128)(2,1)}, u32[]{:S(2)}, u32[]{:S(2)}) %all-to-all-start.2) | async-done | bytes 2293792 | tf_op jit(solution)/shard_map/all_to_all | solution.py:130
  108.7 7.9 %all-to-all-start = ((bf16[32,10,3584]{2,1,0:T(8,128)(2,1)}), bf16[32,10,3584]{2,1,0:T(8,128)(2,1)}, u32[]{:S(2)}, u32[]{:S(2)}) async-start(bf16[32,10,3584]{2,1,0:T(8,128)(2,1)} %pad_maximum_fusion), calls=%async_computation | async-start | bytes 7340032 | tf_op jit(solution)/shard_map/all_to_all | solution.py:130
  116.7 3.1 reshape.163
  119.8 3.4 fusion.6
  123.2 7.3 %convolution_convert_fusion = bf16[320,3584]{1,0:T(8,128)(2,1)} fusion(bf16[1,1,512,3584]{3,2,1,0:T(8,128)(2,1)} %param.19, bf16[320,3584]{1,0:T(8,128)(2,1)S(1)} %reshape.163, bf16[1,1,3584,512]{3,2,1,0:T(8,128)(2,1)} %param.18, f32[320,512]{1,0:T(8,128)S(1)} %fusion.6), kind=kOutput, calls=%fused_computation.4 | convolution fusion | flops 2350940160 | bytes 12582912 | tf_op jit(solution)/shard_map/dot_general | solution.py:51
  130.4 4.4 %reshape.164 = bf16[32,10,3584]{2,1,0:T(8,128)(2,1)} reshape(bf16[320,3584]{1,0:T(8,128)(2,1)} %convolution_convert_fusion) | data formatting | bytes 4587520 | tf_op jit(solution)/shard_map/reshape | solution.py:112
  134.8 63.9 %all-to-all-done = bf16[32,10,3584]{2,1,0:T(8,128)(2,1)} async-done(((bf16[32,10,3584]{2,1,0:T(8,128)(2,1)}), bf16[32,10,3584]{2,1,0:T(8,128)(2,1)}, u32[]{:S(2)}, u32[]{:S(2)}) %all-to-all-start) | async-done | bytes 2293792 | tf_op jit(solution)/shard_map/all_to_all | solution.py:130
  198.8 7.9 %all-to-all-start.3 = ((bf16[32,10,3584]{2,1,0:T(8,128)(2,1)}), bf16[32,10,3584]{2,1,0:T(8,128)(2,1)}, u32[]{:S(2)}, u32[]{:S(2)}) async-start(bf16[32,10,3584]{2,1,0:T(8,128)(2,1)} %reshape.164), calls=%async_computation.3 | async-start | bytes 7340032 | tf_op jit(solution)/shard_map/all_to_all | solution.py:129
  206.7 3.1 reshape.155
  209.9 3.4 fusion.8
  213.2 7.2 %convolution_convert_fusion.1 = bf16[320,3584]{1,0:T(8,128)(2,1)} fusion(bf16[1,1,512,3584]{3,2,1,0:T(8,128)(2,1)} %param.19, bf16[320,3584]{1,0:T(8,128)(2,1)S(1)} %reshape.155, bf16[1,1,3584,512]{3,2,1,0:T(8,128)(2,1)} %param.18, f32[320,512]{1,0:T(8,128)S(1)} %fusion.8), kind=kOutput, calls=%fused_computation.5 | convolution fusion | flops 2350940160 | bytes 12582912 | tf_op jit(solution)/shard_map/dot_general | solution.py:51
  220.4 4.4 %reshape.156 = bf16[32,10,3584]{2,1,0:T(8,128)(2,1)} reshape(bf16[320,3584]{1,0:T(8,128)(2,1)} %convolution_convert_fusion.1) | data formatting | bytes 4587520 | tf_op jit(solution)/shard_map/reshape | solution.py:112
  224.8 64.0 %all-to-all-done.3 = bf16[32,10,3584]{2,1,0:T(8,128)(2,1)} async-done(((bf16[32,10,3584]{2,1,0:T(8,128)(2,1)}), bf16[32,10,3584]{2,1,0:T(8,128)(2,1)}, u32[]{:S(2)}, u32[]{:S(2)}) %all-to-all-start.3) | async-done | bytes 2293792 | tf_op jit(solution)/shard_map/all_to_all | solution.py:129
  288.9 8.0 %all-to-all-start.1 = ((bf16[32,10,3584]{2,1,0:T(8,128)(2,1)}), bf16[32,10,3584]{2,1,0:T(8,128)(2,1)}, u32[]{:S(2)}, u32[]{:S(2)}) async-start(bf16[32,10,3584]{2,1,0:T(8,128)(2,1)} %reshape.156), calls=%async_computation.1 | async-start | bytes 7340032 | tf_op jit(solution)/shard_map/all_to_all | solution.py:129
  302.6 4.4 %fusion.72 = (bf16[32,5,3584]{2,1,0:T(8,128)(2,1)S(1)}, bf16[32,5,3584]{2,1,0:T(8,128)(2,1)}) fusion(bf16[32,10,3584]{2,1,0:T(8,128)(2,1)} %all-to-all-done.3), kind=kLoop, calls=%fused_computation.118 | loop fusion | bytes 4587520 | tf_op jit(solution)/shard_map/slice | solution.py:122
  306.9 1.7 reshape.167
  308.7 2.0 gather_fusion.3
  310.7 1.6 fusion.22
  313.5 65.4 %all-to-all-done.1 = bf16[32,10,3584]{2,1,0:T(8,128)(2,1)} async-done(((bf16[32,10,3584]{2,1,0:T(8,128)(2,1)}), bf16[32,10,3584]{2,1,0:T(8,128)(2,1)}, u32[]{:S(2)}, u32[]{:S(2)}) %all-to-all-start.1) | async-done | bytes 2293792 | tf_op jit(solution)/shard_map/all_to_all | solution.py:129
  378.9 4.9 %fusion.73 = (bf16[32,5,3584]{2,1,0:T(8,128)(2,1)}, bf16[32,5,3584]{2,1,0:T(8,128)(2,1)}) fusion(bf16[32,10,3584]{2,1,0:T(8,128)(2,1)} %all-to-all-done.1), kind=kLoop, calls=%fused_computation.119 | loop fusion | bytes 4587520 | tf_op jit(solution)/shard_map/slice | solution.py:122
  383.8 1.7 reshape.157
  385.5 1.7 reshape.159
  387.2 2.2 gather_fusion.1
  389.4 1.6 fusion.26
  395.9 1.6 fusion.60
  397.5 1.6 fusion.61
  (91 shorter events, 23.7 us)
Async XLA Ops:
  0.6 5.8 %collective-permute-start.3 = (bf16[16,3584]{1,0:T(8,128)(2,1)}, bf16[16,3584]{1,0:T(8,128)(2,1)S(1)}, u32[]{:S(2)}, u32[]{:S(2)}) collective-permute-start(bf16[16,3584]{1,0:T(8,128)(2,1)} %bitcast.107), channel_id=1, source_target_pairs={{0,192},{32,224},{64,0},{96,32},{128,64},{160,96},{192,128},{224,1... | collective-permute-start | bytes 344072 | tf_op jit(solution)/shard_map/ppermute | solution.py:20
  6.7 1.4 collective-permute-start.4
  14.7 11.8 %copy-start.4 = (bf16[1,16,3584]{2,1,0:T(8,128)(2,1)S(1)}, bf16[1,16,3584]{2,1,0:T(8,128)(2,1)}, u32[]{:S(2)}) copy-start(bf16[1,16,3584]{2,1,0:T(8,128)(2,1)} %param.11) | copy-start | bytes 344068
  14.7 94.1 %all-to-all-start.2 = ((bf16[32,10,3584]{2,1,0:T(8,128)(2,1)}), bf16[32,10,3584]{2,1,0:T(8,128)(2,1)}, u32[]{:S(2)}, u32[]{:S(2)}) async-start(bf16[32,10,3584]{2,1,0:T(8,128)(2,1)} %pad_maximum_fusion.1), calls=%async_computation.2 | async-start | bytes 7340032 | tf_op jit(solution)/shard_map/all_to_all | solution.py:130
  26.4 6.6 %collective-permute-start = (bf16[16,3584]{1,0:T(8,128)(2,1)S(1)}, bf16[16,3584]{1,0:T(8,128)(2,1)S(1)}, u32[]{:S(2)}, u32[]{:S(2)}) collective-permute-start(bf16[16,3584]{1,0:T(8,128)(2,1)S(1)} %bitcast.108), channel_id=1, source_target_pairs={{0,64},{32,96},{64,128},{96,160},{128,192},{160,224},{192,0},{224,... | collective-permute-start | bytes 344072 | tf_op jit(solution)/shard_map/ppermute | solution.py:20
  33.1 0.6 copy-start
  33.3 1.4 collective-permute-start.1
  108.7 90.0 %all-to-all-start = ((bf16[32,10,3584]{2,1,0:T(8,128)(2,1)}), bf16[32,10,3584]{2,1,0:T(8,128)(2,1)}, u32[]{:S(2)}, u32[]{:S(2)}) async-start(bf16[32,10,3584]{2,1,0:T(8,128)(2,1)} %pad_maximum_fusion), calls=%async_computation | async-start | bytes 7340032 | tf_op jit(solution)/shard_map/all_to_all | solution.py:130
  198.8 90.1 %all-to-all-start.3 = ((bf16[32,10,3584]{2,1,0:T(8,128)(2,1)}), bf16[32,10,3584]{2,1,0:T(8,128)(2,1)}, u32[]{:S(2)}, u32[]{:S(2)}) async-start(bf16[32,10,3584]{2,1,0:T(8,128)(2,1)} %reshape.164), calls=%async_computation.3 | async-start | bytes 7340032 | tf_op jit(solution)/shard_map/all_to_all | solution.py:129
  288.9 90.1 %all-to-all-start.1 = ((bf16[32,10,3584]{2,1,0:T(8,128)(2,1)}), bf16[32,10,3584]{2,1,0:T(8,128)(2,1)}, u32[]{:S(2)}, u32[]{:S(2)}) async-start(bf16[32,10,3584]{2,1,0:T(8,128)(2,1)} %reshape.156), calls=%async_computation.1 | async-start | bytes 7340032 | tf_op jit(solution)/shard_map/all_to_all | solution.py:129
  313.0 82.9 %collective-permute-start.5 = (bf16[16,3584]{1,0:T(8,128)(2,1)}, bf16[16,3584]{1,0:T(8,128)(2,1)}, u32[]{:S(2)}, u32[]{:S(2)}) collective-permute-start(bf16[16,3584]{1,0:T(8,128)(2,1)} %bitcast.105), channel_id=1, source_target_pairs={{0,32},{32,0},{64,96},{96,64},{128,160},{160,128},{192,224},{224,1... | collective-permute-start | bytes 344072 | tf_op jit(solution)/shard_map/ppermute | solution.py:14
  391.7 5.8 %collective-permute-start.2 = (bf16[16,3584]{1,0:T(8,128)(2,1)}, bf16[16,3584]{1,0:T(8,128)(2,1)}, u32[]{:S(2)}, u32[]{:S(2)}) collective-permute-start(bf16[16,3584]{1,0:T(8,128)(2,1)} %bitcast.106), channel_id=1, source_target_pairs={{0,32},{32,0},{64,96},{96,64},{128,160},{160,128},{192,224},{224,1... | collective-permute-start | bytes 344072 | tf_op jit(solution)/shard_map/ppermute | solution.py:14
  393.0 1.3 copy-start.2
  393.0 1.3 copy-start.3
  394.2 3.3 copy-start.1
where the time goes:
time: 404 us; the launch traced here: 399 us
  waiting for transfers between devices  264 us (65%)
  local copies, waits for them, and re-layouts  48.1 us (12%)
  starting transfers between devices  39.9 us (10%)
  matrix products  28 us (7%)
  other arithmetic  17.8 us (4%)
    all_to_all x2, waiting for transfers between devices, apart_pass(): lax.all_to_all(outgoing, 'expert', split_axis=0, concat_axis=0, tiled=True)  131 us
    all_to_all x2, waiting for transfers between devices, apart_pass(): lax.all_to_all(compute(lax.all_to_all(outgoing, 'expert', split_axis=0, c...  129 us
    all_to_all x2, starting transfers between devices, apart_pass(): lax.all_to_all(outgoing, 'expert', split_axis=0, concat_axis=0, tiled=True)  19.7 us
    all_to_all x2, starting transfers between devices, apart_pass(): lax.all_to_all(compute(lax.all_to_all(outgoing, 'expert', split_axis=0, c...  15.9 us
    dot_general x2, matrix products, expert(): jnp.dot(hidden, down_local, preferred_element_type=jnp.float32)  14.4 us
    slice x2, local copies, waits for them, and re-layouts, finish(): returned[:, :capacity].reshape(-1, width)  9.27 us
    concatenate x2, other arithmetic, begin(): jnp.concatenate([out_own, out_other], axis=1)  9.06 us
    reshape x2, local copies, waits for them, and re-layouts, compute(): expert(flat_rows, gate_local, up_local, down_local).reshape(arrived.shape)  8.82 us
  transfers between devices with their start and end apart: 10, of which 6 were waited for; matrix products, arithmetic and copies ran while one was open for 21% of the time, Pallas kernels for 0%

commit v1 on v0

v1 whole, which is shorter than its diff:
```python
import jax
import jax.numpy as jnp
from jax import lax
from jax.experimental import pallas as pl
from jax.experimental.pallas import tpu as pltpu
from jax.sharding import PartitionSpec as P

MESH = pl.DeviceIdType.MESH
F32 = jnp.float32
BF16 = jnp.bfloat16

WIDTH = 3584
HALF = 512
ROWS = 16
TOP = 8
CAP = 5
CHUNKS = 2
COLS = WIDTH // CHUNKS
FOLD = COLS // 2
ITEMS = 2 * CHUNKS
NX = 4
NZ = 8
OFFSETS = (0, 1, -1, 2, -2, 3, -3, 4)


def parents(chunk):
    return (None, 0, 0, 1, 2, 3, 4, 5 if chunk % 2 == 0 else 6)


def children(chunk, slot):
    return [i for i in range(NZ) if parents(chunk)[i] == slot]


def tiles(width, step, body):
    @pl.loop(0, width // step)
    def _(j):
        body(pl.multiple_of(j * step, step))


def dot(a, b):
    return jnp.dot(a, b, preferred_element_type=F32)


def kernel(
    tok_a, tok_b, ids_a, ids_b, gates_a, gates_b, gate_hbm, up_hbm, down_hbm,
    out_a, out_b,
    wgu, wdn, state, meta, sel, mixw, xg, snd, sndl, xs, fold, acc, hid, yo, yx, yr,
    ret, retl, rb, rbl, ct, rss, rsr,
    w_sem, y_s, y_r, m_s, m_r, ag_s, ag_r, x_s, x_r, ex_s, ex_r, yx_s, yx_r, rt_s, rt_r, rs_s, rs_r,
):
    section = lax.axis_index("section")
    place = lax.axis_index("expert")
    z_at, x_at = place // NX, place % NX
    partner = (section + 1 - 2 * (section % 2), place)

    def along_y(layers):
        return ((section + 2 * layers + 8) % 8, place)

    def along_z(steps):
        return (section, ((z_at + steps + 2 * NZ) % NZ) * NX + x_at)

    def along_x(steps):
        return (section, z_at * NX + (x_at + steps + NX) % NX)

    tokens = (tok_a, tok_b)
    outs = (out_a, out_b)
    sent = []

    def remote(src, dst, send, recv, device):
        return pltpu.make_async_remote_copy(
            src_ref=src, dst_ref=dst, send_sem=send, recv_sem=recv, device_id=device, device_id_type=MESH
        )

    def start(copy):
        copy.start()
        sent.append(copy)

    def y_copy(s):
        return remote(tokens[s].at[0], state.at[s], y_s.at[s], y_r.at[s], along_y(1 if s == 0 else -1))

    def meta_copy(i):
        return remote(
            meta.at[pl.ds(0, ROWS)], meta.at[pl.ds(ROWS * i, ROWS)], m_s.at[i], m_r.at[i], along_z(OFFSETS[i])
        )

    def ag_copy(q, i):
        p = parents(q % CHUNKS)[i]
        return remote(
            xg.at[q, pl.ds(ROWS * p, ROWS)], xg.at[q, pl.ds(ROWS * i, ROWS)],
            ag_s.at[q, i], ag_r.at[q, i], along_z(OFFSETS[i] - OFFSETS[p]),
        )

    def x_copy(q, u, dx):
        sems = (x_s.at[q, u, dx], x_r.at[q, u, dx], along_x(dx))
        rows = pl.ds(16 * dx, 16)
        if u == 2:
            return remote(sndl.at[q, rows], fold.at[q, 0, rows], *sems)
        return remote(snd.at[q, u, rows], xs.at[q, pl.ds(64 * u + 16 * dx, 16)], *sems)

    def ex_copy(q, u):
        sems = (ex_s.at[q, u], ex_r.at[q, u], partner)
        if u == 2:
            return remote(fold.at[q, 0], fold.at[q, 1], *sems)
        return remote(xs.at[q, pl.ds(64 * u, 64)], xs.at[q, pl.ds(128 + 64 * u, 64)], *sems)

    def yx_copy(q):
        return remote(yx.at[q], yr.at[q], yx_s.at[q], yx_r.at[q], partner)

    def rt_copy(q, u, dx):
        sems = (rt_s.at[q, u, dx], rt_r.at[q, u, dx], along_x(-dx))
        rows = pl.ds(16 * dx, 16)
        if u == 2:
            return remote(retl.at[q, rows], rbl.at[q, rows], *sems)
        return remote(ret.at[q, u, rows], rb.at[q, u, rows], *sems)

    def rs_copy(q, i):
        p = parents(q % CHUNKS)[i]
        rows = pl.ds(ROWS * i, ROWS)
        return remote(
            rss.at[q, rows], rsr.at[q, rows], rs_s.at[q, i], rs_r.at[q, i], along_z(OFFSETS[p] - OFFSETS[i])
        )

    loads = [
        pltpu.make_async_copy(gate_hbm.at[0, 0], wgu.at[:, pl.ds(0, HALF)], w_sem.at[0]),
        pltpu.make_async_copy(up_hbm.at[0, 0], wgu.at[:, pl.ds(HALF, HALF)], w_sem.at[1]),
        pltpu.make_async_copy(down_hbm.at[0, 0], wdn, w_sem.at[2]),
    ]
    for load in loads:
        load.start()

    barrier = pltpu.get_barrier_semaphore()
    friends = [along_y(1), along_y(-1), partner]
    friends += [along_z(OFFSETS[i]) for i in range(1, NZ)]
    friends += [along_x(dx) for dx in range(1, NX)]
    for friend in friends:
        pl.semaphore_signal(barrier, inc=1, device_id=friend, device_id_type=MESH)

    lane8 = lax.broadcasted_iota(jnp.int32, (TOP, 128), 1)
    row8 = lax.broadcasted_iota(jnp.int32, (TOP, 128), 0)
    block = jnp.zeros((ROWS, 128), F32)
    for s, (ids_ref, gates_ref) in enumerate(((ids_a, gates_a), (ids_b, gates_b))):
        ids = ids_ref[0, section].astype(F32).astype(BF16)
        gates = gates_ref[0, section]
        high = gates.astype(BF16)
        low = (gates - high.astype(F32)).astype(BF16)
        for j, part in enumerate((ids, high, low)):
            spot = jnp.where(lane8 == row8 + (24 * s + 8 * j), 1.0, 0.0).astype(BF16)
            block = block + dot(part, spot)
    meta[0:ROWS, :] = block.astype(BF16)

    pl.semaphore_wait(barrier, len(friends))

    def y_start(s):
        start(y_copy(s))

    def norm(s):
        y_copy(s).wait_recv()
        values = state[s].astype(F32)
        scale = lax.rsqrt(jnp.mean(values * values, axis=-1, keepdims=True) + 1e-06)
        normed = (values * scale).astype(BF16)
        for c in range(CHUNKS):
            xg[s * CHUNKS + c, 0:ROWS, :] = normed[:, c * COLS:(c + 1) * COLS]

    def z_send(q, slot):
        for i in children(q % CHUNKS, slot):
            start(ag_copy(q, i))

    def z_forward(q, slot):
        ag_copy(q, slot).wait_recv()
        z_send(q, slot)

    def plan():
        for i in range(1, NZ):
            meta_copy(i).wait_recv()
        table = meta[...].astype(F32).T
        lane = lax.broadcasted_iota(jnp.int32, (128, 128), 1)
        row = lax.broadcasted_iota(jnp.int32, (128, 128), 0)
        earlier = jnp.where((row // ROWS == lane // ROWS) & (row < lane), 1.0, 0.0).astype(BF16)
        first = (lax.broadcasted_iota(jnp.int32, (1, 128), 1) // ROWS) * CAP
        for s in range(2):
            ids_t, high_t, low_t = (table[24 * s + 8 * j:24 * s + 8 * j + 8] for j in range(3))
            named, highs, lows = [], [], []
            for dx in range(NX):
                expert_at = (z_at * NX + (x_at + dx) % NX).astype(F32)
                same = jnp.where(ids_t == expert_at, 1.0, 0.0)
                named.append(jnp.sum(same, axis=0, keepdims=True))
                highs.append(jnp.sum(same * high_t, axis=0, keepdims=True))
                lows.append(jnp.sum(same * low_t, axis=0, keepdims=True))
            stacked = jnp.concatenate(named + [jnp.zeros((8 - NX, 128), F32)], axis=0)
            before = dot(stacked.astype(BF16), earlier)
            for u, (least, most, shift) in enumerate(((0, 16, 0), (16, 32, 0), (32, 48, 0), (32, 48, 8))):
                picks = jnp.zeros((128, 128), F32)
                high_w = jnp.zeros((128, 128), F32)
                low_w = jnp.zeros((128, 128), F32)
                for dx in range(NX):
                    spot = first + before[dx:dx + 1].astype(jnp.int32)
                    here = (named[dx] > 0.5) & (spot >= least) & (spot < most)
                    target = jnp.where(here, spot - least + shift + 16 * dx, -1)
                    hit = row == target
                    picks = picks + jnp.where(hit, 1.0, 0.0)
                    high_w = high_w + jnp.where(hit, highs[dx], 0.0)
                    low_w = low_w + jnp.where(hit, lows[dx], 0.0)
                sel[s, u] = picks[0:64].astype(BF16)
                mixw[s, u, 0] = high_w.T.astype(BF16)
                mixw[s, u, 1] = low_w.T.astype(BF16)

    def select(q, u):
        s = q // CHUNKS
        if u == 2:
            def body(at):
                value = dot(sel[s, 2], xg[q, :, pl.ds(at, 128)])
                value = value + dot(sel[s, 3], xg[q, :, pl.ds(FOLD + at, 128)])
                value = value.astype(BF16)
                fold[q, 0, 0:16, pl.ds(at, 128)] = value[0:16]
                sndl[q, 16:64, pl.ds(at, 128)] = value[16:64]
            tiles(FOLD, 128, body)
        else:
            depth = 64 if u == 0 else 112

            def body(at):
                value = dot(sel[s, u][:, 0:depth], xg[q, 0:depth, pl.ds(at, 256)]).astype(BF16)
                xs[q, 64 * u:64 * u + 16, pl.ds(at, 256)] = value[0:16]
                snd[q, u, 16:64, pl.ds(at, 256)] = value[16:64]
            tiles(COLS, 256, body)
        for dx in (2, 1, 3):
            start(x_copy(q, u, dx))

    def exchange(q, u):
        for dx in (1, 3, 2):
            x_copy(q, u, dx).wait_recv()
        start(ex_copy(q, u))

    def gate_up(q):
        s, c = q // CHUNKS, q % CHUNKS
        for u in range(3):
            ex_copy(q, u).wait_recv()

        def unfold(at):
            for h in range(2):
                part = fold[q, h, :, pl.ds(at, 128)].astype(F32)
                left = jnp.concatenate([part[16 * dx:16 * dx + 8] for dx in range(NX)], axis=0)
                right = jnp.concatenate([part[16 * dx + 8:16 * dx + 16] for dx in range(NX)], axis=0)
                xs[q, 256 + 32 * h:288 + 32 * h, pl.ds(at, 128)] = left.astype(BF16)
                xs[q, 256 + 32 * h:288 + 32 * h, pl.ds(FOLD + at, 128)] = right.astype(BF16)
        tiles(FOLD, 128, unfold)

        def body(at):
            value = dot(xs[q], wgu[c * COLS:(c + 1) * COLS, pl.ds(at, 256)])
            if c == 0:
                acc[:, pl.ds(at, 256)] = value
            else:
                acc[:, pl.ds(at, 256)] = acc[:, pl.ds(at, 256)] + value
        tiles(2 * HALF, 256, body)

    def activate(s):
        def body(at):
            gate = acc[:, pl.ds(at, 128)]
            up = acc[:, pl.ds(HALF + at, 128)]
            hid[s, :, pl.ds(at, 128)] = (gate / (1.0 + jnp.exp(-gate)) * up).astype(BF16)
        tiles(HALF, 128, body)

    def down(q):
        s, c = q // CHUNKS, q % CHUNKS

        def body(at):
            value = dot(hid[s], wdn[:, pl.ds(c * COLS + at, 256)])
            yo[q, 0:128, pl.ds(at, 256)] = value[0:128]
            yo[q, 128:160, pl.ds(at, 256)] = value[256:288]
            yx[q, 0:128, pl.ds(at, 256)] = value[128:256].astype(BF16)
            yx[q, 128:160, pl.ds(at, 256)] = value[288:320].astype(BF16)
        tiles(COLS, 256, body)
        start(yx_copy(q))

    def send_back(q):
        yx_copy(q).wait_recv()

        def left(at):
            near = yo[q, 128:160, pl.ds(at, 128)] + yr[q, 128:160, pl.ds(at, 128)].astype(F32)
            far = yo[q, 128:160, pl.ds(FOLD + at, 128)] + yr[q, 128:160, pl.ds(FOLD + at, 128)].astype(F32)
            for dx in range(NX):
                both = jnp.concatenate([near[8 * dx:8 * dx + 8], far[8 * dx:8 * dx + 8]], axis=0).astype(BF16)
                (rbl if dx == 0 else retl)[q, 16 * dx:16 * dx + 16, pl.ds(at, 128)] = both
        tiles(FOLD, 128, left)
        for dx in (2, 1, 3):
            start(rt_copy(q, 2, dx))
        for u in (1, 0):
            def main(at):
                rows = pl.ds(64 * u, 64)
                both = (yo[q, rows, pl.ds(at, 256)] + yr[q, rows, pl.ds(at, 256)].astype(F32)).astype(BF16)
                rb[q, u, 0:16, pl.ds(at, 256)] = both[0:16]
                ret[q, u, 16:64, pl.ds(at, 256)] = both[16:64]
            tiles(COLS, 256, main)
            for dx in (2, 1, 3):
                start(rt_copy(q, u, dx))

    def mix(q, u):
        s = q // CHUNKS
        for dx in (1, 3, 2):
            rt_copy(q, u, dx).wait_recv()

        def weights(k, low, high):
            return jnp.concatenate(
                [mixw[s, k, 0, low:high][:, 0:64], mixw[s, k, 1, low:high][:, 0:64]], axis=0
            )

        if u == 2:
            def body(at):
                rows = rbl[q, :, pl.ds(at, 128)]
                for k, base in ((2, 0), (3, FOLD)):
                    value = dot(weights(k, 96, 128), rows)
                    ct[q, 96:128, pl.ds(base + at, 128)] = value[0:32] + value[32:64]
            tiles(FOLD, 128, body)
        else:
            low, high, shared = (48, 112, 96) if u == 1 else (0, 64, 48)

            def body(at):
                both = dot(weights(u, low, high), rb[q, u, :, pl.ds(at, 256)])
                value = both[0:64] + both[64:128]
                ct[q, low:shared, pl.ds(at, 256)] = value[0:shared - low]
                ct[q, shared:high, pl.ds(at, 256)] = ct[q, shared:high, pl.ds(at, 256)] + value[shared - low:]
            tiles(COLS, 256, body)

    def gathered(q, slot):
        total = ct[q, ROWS * slot:ROWS * (slot + 1)]
        for i in children(q % CHUNKS, slot):
            rs_copy(q, i).wait_recv()
            total = total + rsr[q, ROWS * i:ROWS * (i + 1)].astype(F32)
        return total

    def reduce(q, slot):
        rss[q, ROWS * slot:ROWS * (slot + 1)] = gathered(q, slot).astype(BF16)
        start(rs_copy(q, slot))

    def finish(q):
        s, c = q // CHUNKS, q % CHUNKS
        total = gathered(q, 0) + state[s][:, c * COLS:(c + 1) * COLS].astype(F32)
        outs[s][0, :, c * COLS:(c + 1) * COLS] = total.astype(BF16)

    first, second = range(CHUNKS), range(CHUNKS, ITEMS)

    y_start(0)
    y_start(1)
    for i in range(1, NZ):
        start(meta_copy(i))
    norm(0)
    for q in first:
        z_send(q, 0)
    norm(1)
    plan()

    def step(items, slots):
        for q in items:
            for slot in slots:
                z_forward(q, slot)

    step(first, (1, 2))
    step(first, (3, 4))
    for q in second:
        z_send(q, 0)
    for q in first:
        select(q, 0)
    step(first, (5, 6))
    for q in first:
        select(q, 1)
    step(second, (1, 2))
    step(first, (7,))
    for q in first:
        select(q, 2)
    step(second, (3, 4))
    for q in second:
        select(q, 0)
    for q in first:
        exchange(q, 0)
    step(second, (5, 6))
    for q in second:
        select(q, 1)
    for q in first:
        exchange(q, 1)
    step(second, (7,))
    for q in second:
        select(q, 2)
    for q in first:
        exchange(q, 2)
    loads[0].wait()
    loads[1].wait()
    for q in first:
        gate_up(q)
    activate(0)
    loads[2].wait()
    for q in first:
        down(q)
    for q in first:
        send_back(q)
    for u in range(3):
        for q in second:
            exchange(q, u)
    for q in second:
        gate_up(q)
    activate(1)
    for q in second:
        down(q)
    for q in second:
        send_back(q)
    for q in first:
        mix(q, 2)
        reduce(q, 7)
        mix(q, 1)
        reduce(q, 6)
        mix(q, 0)
    for q in first:
        reduce(q, 5)
        reduce(q, 4)
    for q in second:
        mix(q, 2)
        reduce(q, 7)
    for q in first:
        reduce(q, 3)
        reduce(q, 2)
    for q in second:
        mix(q, 1)
        reduce(q, 6)
    for q in first:
        reduce(q, 1)
    for q in second:
        reduce(q, 5)
        reduce(q, 4)
    for q in second:
        mix(q, 0)
    for q in first:
        finish(q)
    for q in second:
        reduce(q, 3)
        reduce(q, 2)
    for q in second:
        reduce(q, 1)
    for q in second:
        finish(q)
    for copy in sent:
        copy.wait_send()


def body(*args):
    vmem = pl.BlockSpec(memory_space=pltpu.VMEM)
    hbm = pl.BlockSpec(memory_space=pl.ANY)
    dma = pltpu.SemaphoreType.DMA
    q = ITEMS
    state = jax.ShapeDtypeStruct((1, ROWS, WIDTH), BF16)
    return pl.pallas_call(
        kernel,
        out_shape=(state, state),
        in_specs=[vmem] * 6 + [hbm] * 3,
        out_specs=(vmem, vmem),
        scratch_shapes=[
            pltpu.VMEM((WIDTH, 2 * HALF), BF16),
            pltpu.VMEM((HALF, WIDTH), BF16),
            pltpu.VMEM((2, ROWS, WIDTH), BF16),
            pltpu.VMEM((128, 128), BF16),
            pltpu.VMEM((2, 4, 64, 128), BF16),
            pltpu.VMEM((2, 4, 2, 128, 128), BF16),
            pltpu.VMEM((q, 128, COLS), BF16),
            pltpu.VMEM((q, 2, 64, COLS), BF16),
            pltpu.VMEM((q, 64, FOLD), BF16),
            pltpu.VMEM((q, 320, COLS), BF16),
            pltpu.VMEM((q, 2, 64, FOLD), BF16),
            pltpu.VMEM((320, 2 * HALF), F32),
            pltpu.VMEM((2, 320, HALF), BF16),
            pltpu.VMEM((q, 160, COLS), F32),
            pltpu.VMEM((q, 160, COLS), BF16),
            pltpu.VMEM((q, 160, COLS), BF16),
            pltpu.VMEM((q, 2, 64, COLS), BF16),
            pltpu.VMEM((q, 64, FOLD), BF16),
            pltpu.VMEM((q, 2, 64, COLS), BF16),
            pltpu.VMEM((q, 64, FOLD), BF16),
            pltpu.VMEM((q, 128, COLS), F32),
            pltpu.VMEM((q, 128, COLS), BF16),
            pltpu.VMEM((q, 128, COLS), BF16),
            dma((3,)),
            dma((2,)), dma((2,)),
            dma((NZ,)), dma((NZ,)),
            dma((q, NZ)), dma((q, NZ)),
            dma((q, 3, NX)), dma((q, 3, NX)),
            dma((q, 3)), dma((q, 3)),
            dma((q,)), dma((q,)),
            dma((q, 3, NX)), dma((q, 3, NX)),
            dma((q, NZ)), dma((q, NZ)),
        ],
        compiler_params=pltpu.CompilerParams(
            collective_id=0, has_side_effects=True, vmem_limit_bytes=60 * 2**20
        ),
        name="routed_layer",
    )(*args)


def solution(mesh):
    states = P("section", "expert", None)
    routes = P(None, None, "expert", None)
    weights = P("section", "expert", None, None)
    return jax.shard_map(
        body,
        mesh=mesh,
        in_specs=(states, states, routes, routes, routes, routes, weights, weights, weights),
        out_specs=(states, states),
        check_vma=False,
    )
```

time: 404 us -> 110 us (0.27); the launches traced: 399 us -> 110 us
  waiting for transfers between devices: 264 us -> 0 us
  Pallas kernels: 0 us -> 100 us
  starting transfers between devices: 39.9 us -> 0 us
  local copies, waits for them, and re-layouts: 48.1 us -> 8.97 us
  matrix products: 28 us -> 0 us
  other arithmetic: 17.8 us -> 0 us
    all_to_all x4 -> x0, waiting for transfers between devices: 261 us -> none  [the longest x2 131 us: apart_pass(): lax.all_to_all(outgoing, 'expert', split_axis=0, concat_axis=0, tiled=True)]
    pallas_call x0 -> x1, Pallas kernels: none -> 100 us  [body(): pl.pallas_call(kernel, out_shape=(state, state), in_specs=[vmem] * 6 + [h...]
    all_to_all x4 -> x0, starting transfers between devices: 35.6 us -> none  [the longest x2 19.7 us: apart_pass(): lax.all_to_all(outgoing, 'expert', split_axis=0, concat_axis=0, tiled=True)]
    dot_general x12 -> x0, matrix products: 28 us -> none  [the longest x2 14.4 us: expert(): jnp.dot(hidden, down_local, preferred_element_type=jnp.float32)]
    reshape x12 -> x0, local copies, waits for them, and re-layouts: 24.7 us -> none  [the longest x2 8.82 us: compute(): expert(flat_rows, gate_local, up_local, down_local).reshape(arrived.shape)]
    slice x2 -> x0, local copies, waits for them, and re-layouts: 9.27 us -> none  [finish(): returned[:, :capacity].reshape(-1, width)]
    concatenate x2 -> x0, other arithmetic: 9.06 us -> none  [begin(): jnp.concatenate([out_own, out_other], axis=1)]
    unnamed x10 -> x6, local copies, waits for them, and re-layouts: 0.3 us -> 8.97 us
  transfers between devices with their start and end apart: 10 -> 0, of which waited for: 6 -> 0; matrix products, arithmetic and copies ran while one was open for 21% -> 0% of each run, Pallas kernels for 0% -> 0%
where the time goes in v1:
time: 110 us
  Pallas kernels  100 us (91%)
  local copies, waits for them, and re-layouts  8.97 us (8%)
    pallas_call x1, Pallas kernels, body(): pl.pallas_call(kernel, out_shape=(state, state), in_specs=[vmem] * 6 + [h...  100 us
    unnamed x6, local copies, waits for them, and re-layouts  8.97 us

profile of v1, /device:TPU:4, one launch (start us, length us, event | category | flops | bytes accessed | tf_op | source)
XLA Modules:
  0.0 109.7 jit_solution(3678759649124480493)
XLA Ops:
  0.6 1.5 %copy.11.ids_a = s32[1,8,16,8]{3,2,1,0:T(8,128)} copy(s32[1,8,16,8]{2,3,1,0:T(8,128)} %param.11) | data formatting | bytes 8192 | tf_op args[2]
  2.1 1.5 %copy.12.ids_b = s32[1,8,16,8]{3,2,1,0:T(8,128)} copy(s32[1,8,16,8]{2,3,1,0:T(8,128)} %param.12) | data formatting | bytes 8192 | tf_op args[3]
  3.6 1.5 %copy.13.gates_a = f32[1,8,16,8]{3,2,1,0:T(8,128)} copy(f32[1,8,16,8]{2,3,1,0:T(8,128)} %param.13) | data formatting | bytes 8192 | tf_op args[4]
  5.0 1.5 %copy.14.gates_b = f32[1,8,16,8]{3,2,1,0:T(8,128)} copy(f32[1,8,16,8]{2,3,1,0:T(8,128)} %param.14) | data formatting | bytes 8192 | tf_op args[5]
  6.5 100.1 %routed_layer.1 = (bf16[1,16,3584]{2,1,0:T(8,128)(2,1)}, bf16[1,16,3584]{2,1,0:T(8,128)(2,1)}) custom-call(bf16[1,16,3584]{2,1,0:T(8,128)(2,1)} %tok_a.1, bf16[1,16,3584]{2,1,0:T(8,128)(2,1)} %tok_b.1, s32[1,8,16,8]{3,2,1,0:T(8,128)} %copy.11.ids_a, s32[1,8,16,8]{3,2,1,0:T(8,128)} %copy.12.ids_b, f32[1,8,16,8]{3,2,1,0:T(8,128)} %copy.13.gates_a, ...), custom_call_target="tpu_custom_call" | custom-call | tf_op jit(solution)/shard_map/routed_layer/pallas_call | solution.py:448
  106.6 1.6 %copy.17 = bf16[1,16,3584]{2,1,0:T(8,128)(2,1)} copy(bf16[1,16,3584]{2,1,0:T(8,128)(2,1)} %get-tuple-element.4) | data formatting | bytes 229376
  108.2 1.6 %copy.18 = bf16[1,16,3584]{2,1,0:T(8,128)(2,1)} copy(bf16[1,16,3584]{2,1,0:T(8,128)(2,1)} %get-tuple-element.5) | data formatting | bytes 229376

commit v2 on v1

--- a/solution.py
+++ b/solution.py
@@ -1,3 +1,5 @@
+import functools
+
 import jax
 import jax.numpy as jnp
 from jax import lax
@@ -23,12 +25,102 @@
 OFFSETS = (0, 1, -1, 2, -2, 3, -3, 4)
 
 
-def parents(chunk):
-    return (None, 0, 0, 1, 2, 3, 4, 5 if chunk % 2 == 0 else 6)
-
-
-def children(chunk, slot):
-    return [i for i in range(NZ) if parents(chunk)[i] == slot]
+RING = ((None, 0, 0, 1, 2, 3, 4, 5), (None, 0, 0, 1, 2, 3, 4, 6))
+TREE = (None, 0, 0, 0, 0, 3, 4, 3)
+
+ORDER = (
+    ("first", ((0,), (2,),)),
+    ("plan", ((),)),
+    ("first", ((1,), (3,),)),
+    ("forward", ((0, 1), (0, 2), (0, 3),)),
+    ("select", ((0, 0),)),
+    ("forward", ((0, 4), (2, 1), (2, 2), (1, 1), (1, 2),)),
+    ("exchange", ((0, 0),)),
+    ("forward", ((1, 3),)),
+    ("select", ((1, 0),)),
+    ("forward", ((1, 4), (3, 1), (3, 2), (0, 5), (0, 6),)),
+    ("select", ((0, 1),)),
+    ("forward", ((2, 4), (0, 7),)),
+    ("select", ((0, 2),)),
+    ("forward", ((1, 6),)),
+    ("exchange", ((1, 0),)),
+    ("forward", ((2, 3),)),
+    ("select", ((2, 0),)),
+    ("forward", ((3, 4), (1, 5),)),
+    ("select", ((1, 1),)),
+    ("forward", ((2, 6),)),
+    ("exchange", ((0, 1), (0, 2),)),
+    ("gate_up", ((0, 0),)),
+    ("forward", ((1, 7),)),
+    ("select", ((1, 2),)),
+    ("forward", ((3, 6),)),
+    ("gate_up", ((0, 1),)),
+    ("forward", ((3, 3),)),
+    ("select", ((3, 0),)),
+    ("exchange", ((2, 0),)),
+    ("forward", ((2, 5),)),
+    ("select", ((2, 1),)),
+    ("exchange", ((1, 1),)),
+    ("forward", ((3, 7),)),
+    ("exchange", ((1, 2),)),
+    ("forward", ((3, 5),)),
+    ("select", ((3, 1), (3, 2),)),
+    ("gate_up", ((1, 0),)),
+    ("forward", ((2, 7),)),
+    ("select", ((2, 2),)),
+    ("gate_up", ((1, 1),)),
+    ("exchange", ((3, 0),)),
+    ("activate", ((0,),)),
+    ("down", ((0, 0), (0, 1), (1, 0), (1, 1),)),
+    ("exchange", ((2, 1),)),
+    ("send_back", ((0, 2), (0, 0), (0, 1), (1, 2), (1, 0), (1, 1),)),
+    ("exchange", ((3, 1), (3, 2), (2, 2),)),
+    ("gate_up", ((2, 0),)),
+    ("mix", ((0, 2),)),
+    ("reduce", ((0, 7),)),
+    ("gate_up", ((2, 1), (3, 0), (3, 1),)),
+    ("activate", ((1,),)),
+    ("down", ((2, 0), (2, 1), (3, 0), (3, 1),)),
+    ("mix", ((0, 1),)),
+    ("reduce", ((0, 5), (0, 6),)),
+    ("mix", ((0, 0),)),
+    ("send_back", ((2, 2), (2, 0),)),
+    ("mix", ((1, 2),)),
+    ("reduce", ((1, 7),)),
+    ("send_back", ((2, 1), (3, 2), (3, 0), (3, 1),)),
+    ("reduce", ((0, 3), (0, 4),)),
+    ("mix", ((1, 1),)),
+    ("reduce", ((1, 5), (1, 6),)),
+    ("mix", ((1, 0),)),
+    ("reduce", ((0, 1), (0, 2),)),
+    ("mix", ((2, 2),)),
+    ("reduce", ((2, 7), (1, 3), (1, 4),)),
+    ("finish", ((0,),)),
+    ("mix", ((2, 1),)),
+    ("reduce", ((2, 5), (2, 6),)),
+    ("mix", ((2, 0), (3, 2),)),
+    ("reduce", ((1, 1), (1, 2), (3, 7), (2, 3), (2, 4),)),
+    ("finish", ((1,),)),
+    ("mix", ((3, 1),)),
+    ("reduce", ((3, 5), (3, 6),)),
+    ("mix", ((3, 0),)),
+    ("reduce", ((3, 1), (3, 2), (2, 2), (2, 1), (3, 3), (3, 4),)),
+    ("finish", ((2,), (3,),)),
+)
+DIRECT_OUT = (0, 1)
+DIRECT_BACK = (3,)
+
+
+def out_parents(q):
+    return TREE if q in DIRECT_OUT else RING[q % 2]
+
+
+def back_parents(q):
+    return TREE if q in DIRECT_BACK else RING[q % 2]
+
+
+def below(parents, slot):
+    return [i for i in range(NZ) if parents[i] == slot]
 
 
 def tiles(width, step, body):
@@ -44,9 +136,9 @@
 def kernel(
     tok_a, tok_b, ids_a, ids_b, gates_a, gates_b, gate_hbm, up_hbm, down_hbm,
     out_a, out_b,
-    wgu, wdn, state, meta, sel, mixw, xg, snd, sndl, xs, fold, acc, hid, yo, yx, yr,
+    wgu, wdn, state, near, meta, sel, mixw, xg, snd, sndl, xs, fold, acc, hid, yo, yx, yr,
     ret, retl, rb, rbl, ct, rss, rsr,
-    w_sem, y_s, y_r, m_s, m_r, ag_s, ag_r, x_s, x_r, ex_s, ex_r, yx_s, yx_r, rt_s, rt_r, rs_s, rs_r,
+    w_sem, y_s, y_r, yn_s, yn_r, m_s, m_r, ag_s, ag_r, x_s, x_r, ex_s, ex_r, yx_s, yx_r, rt_s, rt_r, rs_s, rs_r,
 ):
     section = lax.axis_index("section")
     place = lax.axis_index("expert")
@@ -65,6 +157,8 @@
     tokens = (tok_a, tok_b)
     outs = (out_a, out_b)
     sent = []
+    loaded = set()
+    arrived = set()
 
     def remote(src, dst, send, recv, device):
         return pltpu.make_async_remote_copy(
@@ -78,13 +172,18 @@
     def y_copy(s):
         return remote(tokens[s].at[0], state.at[s], y_s.at[s], y_r.at[s], along_y(1 if s == 0 else -1))
 
+    def yn_copy(q):
+        return remote(
+            near.at[q], xg.at[q, pl.ds(0, ROWS)], yn_s.at[q], yn_r.at[q], along_y(1 if q < CHUNKS else -1)
+        )
+
     def meta_copy(i):
         return remote(
             meta.at[pl.ds(0, ROWS)], meta.at[pl.ds(ROWS * i, ROWS)], m_s.at[i], m_r.at[i], along_z(OFFSETS[i])
         )
 
     def ag_copy(q, i):
-        p = parents(q % CHUNKS)[i]
+        p = out_parents(q)[i]
         return remote(
             xg.at[q, pl.ds(ROWS * p, ROWS)], xg.at[q, pl.ds(ROWS * i, ROWS)],
             ag_s.at[q, i], ag_r.at[q, i], along_z(OFFSETS[i] - OFFSETS[p]),
@@ -114,7 +213,7 @@
         return remote(ret.at[q, u, rows], rb.at[q, u, rows], *sems)
 
     def rs_copy(q, i):
-        p = parents(q % CHUNKS)[i]
+        p = back_parents(q)[i]
         rows = pl.ds(ROWS * i, ROWS)
         return remote(
             rss.at[q, rows], rsr.at[q, rows], rs_s.at[q, i], rs_r.at[q, i], along_z(OFFSETS[p] - OFFSETS[i])
@@ -145,27 +244,25 @@
         low = (gates - high.astype(F32)).astype(BF16)
         for j, part in enumerate((ids, high, low)):
             spot = jnp.where(lane8 == row8 + (24 * s + 8 * j), 1.0, 0.0).astype(BF16)
-            block = block + dot(part, spot)
+            block = block + lax.dot_general(part, spot, (((0,), (0,)), ((), ())), preferred_element_type=F32)
     meta[0:ROWS, :] = block.astype(BF16)
 
-    pl.semaphore_wait(barrier, len(friends))
-
-    def y_start(s):
-        start(y_copy(s))
-
     def norm(s):
-        y_copy(s).wait_recv()
-        values = state[s].astype(F32)
+        values = tokens[s][0].astype(F32)
         scale = lax.rsqrt(jnp.mean(values * values, axis=-1, keepdims=True) + 1e-06)
         normed = (values * scale).astype(BF16)
         for c in range(CHUNKS):
-            xg[s * CHUNKS + c, 0:ROWS, :] = normed[:, c * COLS:(c + 1) * COLS]
+            near[s * CHUNKS + c] = normed[:, c * COLS:(c + 1) * COLS]
+
+    def first(q):
+        yn_copy(q).wait_recv()
+        z_send(q, 0)
 
     def z_send(q, slot):
-        for i in children(q % CHUNKS, slot):
+        for i in below(out_parents(q), slot):
             start(ag_copy(q, i))
 
-    def z_forward(q, slot):
+    def forward(q, slot):
         ag_copy(q, slot).wait_recv()
         z_send(q, slot)
 
@@ -207,21 +304,15 @@
     def select(q, u):
         s = q // CHUNKS
         if u == 2:
-            def body(at):
-                value = dot(sel[s, 2], xg[q, :, pl.ds(at, 128)])
-                value = value + dot(sel[s, 3], xg[q, :, pl.ds(FOLD + at, 128)])
-                value = value.astype(BF16)
-                fold[q, 0, 0:16, pl.ds(at, 128)] = value[0:16]
-                sndl[q, 16:64, pl.ds(at, 128)] = value[16:64]
-            tiles(FOLD, 128, body)
+            value = dot(sel[s, 2], xg[q, :, 0:FOLD]) + dot(sel[s, 3], xg[q, :, FOLD:COLS])
+            value = value.astype(BF16)
+            fold[q, 0, 0:16] = value[0:16]
+            sndl[q, 16:64] = value[16:64]
         else:
             depth = 64 if u == 0 else 112
-
-            def body(at):
-                value = dot(sel[s, u][:, 0:depth], xg[q, 0:depth, pl.ds(at, 256)]).astype(BF16)
-                xs[q, 64 * u:64 * u + 16, pl.ds(at, 256)] = value[0:16]
-                snd[q, u, 16:64, pl.ds(at, 256)] = value[16:64]
-            tiles(COLS, 256, body)
+            value = dot(sel[s, u][:, 0:depth], xg[q, 0:depth]).astype(BF16)
+            xs[q, 64 * u:64 * u + 16] = value[0:16]
+            snd[q, u, 16:64] = value[16:64]
         for dx in (2, 1, 3):
             start(x_copy(q, u, dx))
 
@@ -230,27 +321,28 @@
             x_copy(q, u, dx).wait_recv()
         start(ex_copy(q, u))
 
-    def gate_up(q):
-        s, c = q // CHUNKS, q % CHUNKS
+    def gate_up(q, part):
+        c = q % CHUNKS
+        if part == 0:
+            unfold(q)
+        wait_load(part)
+
+        cols = pl.ds(part * HALF, HALF)
+        value = dot(xs[q], wgu[c * COLS:(c + 1) * COLS, cols])
+        acc[:, cols] = value if c == 0 else acc[:, cols] + value
+
+    def unfold(q):
         for u in range(3):
             ex_copy(q, u).wait_recv()
 
-        def unfold(at):
+        def body(at):
             for h in range(2):
                 part = fold[q, h, :, pl.ds(at, 128)].astype(F32)
                 left = jnp.concatenate([part[16 * dx:16 * dx + 8] for dx in range(NX)], axis=0)
                 right = jnp.concatenate([part[16 * dx + 8:16 * dx + 16] for dx in range(NX)], axis=0)
                 xs[q, 256 + 32 * h:288 + 32 * h, pl.ds(at, 128)] = left.astype(BF16)
                 xs[q, 256 + 32 * h:288 + 32 * h, pl.ds(FOLD + at, 128)] = right.astype(BF16)
-        tiles(FOLD, 128, unfold)
-
-        def body(at):
-            value = dot(xs[q], wgu[c * COLS:(c + 1) * COLS, pl.ds(at, 256)])
-            if c == 0:
-                acc[:, pl.ds(at, 256)] = value
-            else:
-                acc[:, pl.ds(at, 256)] = acc[:, pl.ds(at, 256)] + value
-        tiles(2 * HALF, 256, body)
+        tiles(FOLD, 128, body)
 
     def activate(s):
         def body(at):
@@ -259,39 +351,39 @@
             hid[s, :, pl.ds(at, 128)] = (gate / (1.0 + jnp.exp(-gate)) * up).astype(BF16)
         tiles(HALF, 128, body)
 
-    def down(q):
+    def down(q, part):
         s, c = q // CHUNKS, q % CHUNKS
-
-        def body(at):
-            value = dot(hid[s], wdn[:, pl.ds(c * COLS + at, 256)])
-            yo[q, 0:128, pl.ds(at, 256)] = value[0:128]
-            yo[q, 128:160, pl.ds(at, 256)] = value[256:288]
-            yx[q, 0:128, pl.ds(at, 256)] = value[128:256].astype(BF16)
-            yx[q, 128:160, pl.ds(at, 256)] = value[288:320].astype(BF16)
-        tiles(COLS, 256, body)
-        start(yx_copy(q))
-
-    def send_back(q):
-        yx_copy(q).wait_recv()
-
-        def left(at):
-            near = yo[q, 128:160, pl.ds(at, 128)] + yr[q, 128:160, pl.ds(at, 128)].astype(F32)
-            far = yo[q, 128:160, pl.ds(FOLD + at, 128)] + yr[q, 128:160, pl.ds(FOLD + at, 128)].astype(F32)
-            for dx in range(NX):
-                both = jnp.concatenate([near[8 * dx:8 * dx + 8], far[8 * dx:8 * dx + 8]], axis=0).astype(BF16)
-                (rbl if dx == 0 else retl)[q, 16 * dx:16 * dx + 16, pl.ds(at, 128)] = both
-        tiles(FOLD, 128, left)
-        for dx in (2, 1, 3):
-            start(rt_copy(q, 2, dx))
-        for u in (1, 0):
-            def main(at):
+        wait_load(2)
+        for j in range(4 * part, 4 + 3 * part):
+            value = dot(hid[s], wdn[:, c * COLS + 256 * j:c * COLS + 256 * (j + 1)])
+            cols = pl.ds(256 * j, 256)
+            yo[q, 0:128, cols] = value[0:128]
+            yo[q, 128:160, cols] = value[256:288]
+            yx[q, 0:128, cols] = value[128:256].astype(BF16)
+            yx[q, 128:160, cols] = value[288:320].astype(BF16)
+        if part == 1:
+            start(yx_copy(q))
+
+    def send_back(q, u):
+        if u == 2:
+            yx_copy(q).wait_recv()
+
+            def body(at):
+                near = yo[q, 128:160, pl.ds(at, 128)] + yr[q, 128:160, pl.ds(at, 128)].astype(F32)
+                far = yo[q, 128:160, pl.ds(FOLD + at, 128)] + yr[q, 128:160, pl.ds(FOLD + at, 128)].astype(F32)
+                for dx in range(NX):
+                    both = jnp.concatenate([near[8 * dx:8 * dx + 8], far[8 * dx:8 * dx + 8]], axis=0).astype(BF16)
+                    (rbl if dx == 0 else retl)[q, 16 * dx:16 * dx + 16, pl.ds(at, 128)] = both
+            tiles(FOLD, 128, body)
+        else:
+            def body(at):
                 rows = pl.ds(64 * u, 64)
                 both = (yo[q, rows, pl.ds(at, 256)] + yr[q, rows, pl.ds(at, 256)].astype(F32)).astype(BF16)
                 rb[q, u, 0:16, pl.ds(at, 256)] = both[0:16]
                 ret[q, u, 16:64, pl.ds(at, 256)] = both[16:64]
-            tiles(COLS, 256, main)
-            for dx in (2, 1, 3):
-                start(rt_copy(q, u, dx))
+            tiles(COLS, 256, body)
+        for dx in (2, 1, 3):
+            start(rt_copy(q, u, dx))
 
     def mix(q, u):
         s = q // CHUNKS
@@ -304,25 +396,20 @@
             )
 
         if u == 2:
-            def body(at):
-                rows = rbl[q, :, pl.ds(at, 128)]
-                for k, base in ((2, 0), (3, FOLD)):
-                    value = dot(weights(k, 96, 128), rows)
-                    ct[q, 96:128, pl.ds(base + at, 128)] = value[0:32] + value[32:64]
-            tiles(FOLD, 128, body)
+            for k, base in ((2, 0), (3, FOLD)):
+                value = dot(weights(k, 96, 128), rbl[q])
+                ct[q, 96:128, base:base + FOLD] = value[0:32] + value[32:64]
         else:
             low, high, shared = (48, 112, 96) if u == 1 else (0, 64, 48)
-
-            def body(at):
-                both = dot(weights(u, low, high), rb[q, u, :, pl.ds(at, 256)])
+            for base in (0, FOLD):
+                both = dot(weights(u, low, high), rb[q, u, :, base:base + FOLD])
                 value = both[0:64] + both[64:128]
-                ct[q, low:shared, pl.ds(at, 256)] = value[0:shared - low]
-                ct[q, shared:high, pl.ds(at, 256)] = ct[q, shared:high, pl.ds(at, 256)] + value[shared - low:]
-            tiles(COLS, 256, body)
+                ct[q, low:shared, base:base + FOLD] = value[0:shared - low]
+                ct[q, shared:high, base:base + FOLD] = ct[q, shared:high, base:base + FOLD] + value[shared - low:]
 
     def gathered(q, slot):
         total = ct[q, ROWS * slot:ROWS * (slot + 1)]
-        for i in children(q % CHUNKS, slot):
+        for i in below(back_parents(q), slot):
             rs_copy(q, i).wait_recv()
             total = total + rsr[q, ROWS * i:ROWS * (i + 1)].astype(F32)
         return total
@@ -333,113 +420,49 @@
 
     def finish(q):
         s, c = q // CHUNKS, q % CHUNKS
+        if s not in arrived:
+            y_copy(s).wait_recv()
+            arrived.add(s)
         total = gathered(q, 0) + state[s][:, c * COLS:(c + 1) * COLS].astype(F32)
         outs[s][0, :, c * COLS:(c + 1) * COLS] = total.astype(BF16)
 
-    first, second = range(CHUNKS), range(CHUNKS, ITEMS)
-
-    y_start(0)
-    y_start(1)
+    def wait_load(i):
+        if i not in loaded:
+            loads[i].wait()
+            loaded.add(i)
+
+    norm(0)
+    norm(1)
+    pl.semaphore_wait(barrier, len(friends))
+    for q in range(ITEMS):
+        start(yn_copy(q))
     for i in range(1, NZ):
         start(meta_copy(i))
-    norm(0)
-    for q in first:
-        z_send(q, 0)
-    norm(1)
-    plan()
-
-    def step(items, slots):
-        for q in items:
-            for slot in slots:
-                z_forward(q, slot)
-
-    step(first, (1, 2))
-    step(first, (3, 4))
-    for q in second:
-        z_send(q, 0)
-    for q in first:
-        select(q, 0)
-    step(first, (5, 6))
-    for q in first:
-        select(q, 1)
-    step(second, (1, 2))
-    step(first, (7,))
-    for q in first:
-        select(q, 2)
-    step(second, (3, 4))
-    for q in second:
-        select(q, 0)
-    for q in first:
-        exchange(q, 0)
-    step(second, (5, 6))
-    for q in second:
-        select(q, 1)
-    for q in first:
-        exchange(q, 1)
-    step(second, (7,))
-    for q in second:
-        select(q, 2)
-    for q in first:
-        exchange(q, 2)
-    loads[0].wait()
-    loads[1].wait()
-    for q in first:
-        gate_up(q)
-    activate(0)
-    loads[2].wait()
-    for q in first:
-        down(q)
-    for q in first:
-        send_back(q)
-    for u in range(3):
-        for q in second:
-            exchange(q, u)
-    for q in second:
-        gate_up(q)
-    activate(1)
-    for q in second:
-        down(q)
-    for q in second:
-        send_back(q)
-    for q in first:
-        mix(q, 2)
-        reduce(q, 7)
-        mix(q, 1)
-        reduce(q, 6)
-        mix(q, 0)
-    for q in first:
-        reduce(q, 5)
-        reduce(q, 4)
-    for q in second:
-        mix(q, 2)
-        reduce(q, 7)
-    for q in first:
-        reduce(q, 3)
-        reduce(q, 2)
-    for q in second:
-        mix(q, 1)
-        reduce(q, 6)
-    for q in first:
-        reduce(q, 1)
-    for q in second:
-        reduce(q, 5)
-        reduce(q, 4)
-    for q in second:
-        mix(q, 0)
-    for q in first:
-        finish(q)
-    for q in second:
-        reduce(q, 3)
-        reduce(q, 2)
-    for q in second:
-        reduce(q, 1)
-    for q in second:
-        finish(q)
+    for s in range(2):
+        start(y_copy(s))
+    known = dict(
+        first=first, plan=plan, forward=forward, select=select, exchange=exchange, gate_up=gate_up,
+        activate=activate, down=down, send_back=send_back, mix=mix, reduce=reduce, finish=finish,
+    )
+    steps = [functools.partial(known[name], *which) for name, turns in ORDER for which in turns]
+    for step in steps:
+        step()
     for copy in sent:
         copy.wait_send()
 
 
-def body(*args):
+def hand_over(a_ref, b_ref, out_a, out_b, sems):
+    copies = [
+        pltpu.make_async_copy(a_ref, out_a, sems.at[0]),
+        pltpu.make_async_copy(b_ref, out_b, sems.at[1]),
+    ]
+    for copy in copies:
+        copy.start()
+    for copy in copies:
+        copy.wait()
+
+
+def layer(*args):
     vmem = pl.BlockSpec(memory_space=pltpu.VMEM)
     hbm = pl.BlockSpec(memory_space=pl.ANY)
     dma = pltpu.SemaphoreType.DMA
@@ -454,6 +477,7 @@
             pltpu.VMEM((WIDTH, 2 * HALF), BF16),
             pltpu.VMEM((HALF, WIDTH), BF16),
             pltpu.VMEM((2, ROWS, WIDTH), BF16),
+            pltpu.VMEM((q, ROWS, COLS), BF16),
             pltpu.VMEM((128, 128), BF16),
             pltpu.VMEM((2, 4, 64, 128), BF16),
             pltpu.VMEM((2, 4, 2, 128, 128), BF16),
@@ -476,6 +500,7 @@
             pltpu.VMEM((q, 128, COLS), BF16),
             dma((3,)),
             dma((2,)), dma((2,)),
+            dma((q,)), dma((q,)),
             dma((NZ,)), dma((NZ,)),
             dma((q, NZ)), dma((q, NZ)),
             dma((q, 3, NX)), dma((q, 3, NX)),
@@ -491,6 +516,19 @@
     )(*args)
 
 
+def body(tok_a, tok_b, ids_a, ids_b, gates_a, gates_b, gate_proj, up_proj, down_proj):
+    small = [jnp.transpose(v, (0, 1, 3, 2)) for v in (ids_a, ids_b, gates_a, gates_b)]
+    done = layer(tok_a, tok_b, *small, gate_proj, up_proj, down_proj)
+    return pl.pallas_call(
+        hand_over,
+        out_shape=tuple(jax.ShapeDtypeStruct(v.shape, v.dtype) for v in done),
+        in_specs=[pl.BlockSpec(memory_space=pl.ANY)] * 2,
+        out_specs=(pl.BlockSpec(memory_space=pl.ANY),) * 2,
+        scratch_shapes=[pltpu.SemaphoreType.DMA((2,))],
+        name="hand_over",
+    )(*done)
+
+
 def solution(mesh):
     states = P("section", "expert", None)
     routes = P(None, None, "expert", None)

time: 110 us -> 97.5 us (0.89)
  local copies, waits for them, and re-layouts: 8.97 us -> 0 us
  Pallas kernels: 100 us -> 95.7 us
    unnamed x6 -> x0, local copies, waits for them, and re-layouts: 8.97 us -> none
    pallas_call x1 -> x2, Pallas kernels: 100 us -> 95.7 us  [the longest x1 87.7 us: layer(): pl.pallas_call(kernel, out_shape=(state, state), in_specs=[vmem] * 6 + [h...]
where the time goes in v2:
time: 97.5 us; the launch traced here: 96.4 us
  Pallas kernels  95.7 us (98%)
    pallas_call x1, Pallas kernels, layer(): pl.pallas_call(kernel, out_shape=(state, state), in_specs=[vmem] * 6 + [h...  87.7 us
    pallas_call x1, Pallas kernels, body(): pl.pallas_call(hand_over, out_shape=tuple((jax.ShapeDtypeStruct(v.shape,...  8.07 us

profile of v2, /device:TPU:4, one launch (start us, length us, event | category | flops | bytes accessed | tf_op | source)
XLA Modules:
  0.0 96.4 jit_solution(1665142666266598161)
XLA Ops:
  0.6 87.7 %routed_layer.1 = (bf16[1,16,3584]{2,1,0:T(8,128)(2,1)}, bf16[1,16,3584]{2,1,0:T(8,128)(2,1)}) custom-call(bf16[1,16,3584]{2,1,0:T(8,128)(2,1)} %tok_a.1, bf16[1,16,3584]{2,1,0:T(8,128)(2,1)} %tok_b.1, s32[1,8,8,16]{3,2,1,0:T(8,128)} %bitcast.4, s32[1,8,8,16]{3,2,1,0:T(8,128)} %bitcast.5, f32[1,8,8,16]{3,2,1,0:T(8,128)} %bitcast.6, f32[1,8,8,16]{3,2,1,0:T(8,128)} %bitcast.7, ...), custom_call_target="tpu_custom_call" | custom-call | tf_op jit(solution)/shard_map/routed_layer/pallas_call | solution.py:471
  88.3 8.1 %hand_over.1 = (bf16[1,16,3584]{2,1,0:T(8,128)(2,1)}, bf16[1,16,3584]{2,1,0:T(8,128)(2,1)}) custom-call(bf16[1,16,3584]{2,1,0:T(8,128)(2,1)} %get-tuple-element.4.a_ref, bf16[1,16,3584]{2,1,0:T(8,128)(2,1)} %get-tuple-element.5.b_ref), custom_call_target="tpu_custom_call" | custom-call | tf_op jit(solution)/shard_map/hand_over/pallas_call | solution.py:522

commit v3 on v2

v3 whole, which is shorter than its diff:
```python
import functools

import jax
import jax.numpy as jnp
from jax import lax
from jax.experimental import pallas as pl
from jax.experimental.pallas import tpu as pltpu
from jax.sharding import PartitionSpec as P

MESH = pl.DeviceIdType.MESH
F32 = jnp.float32
BF16 = jnp.bfloat16

WIDTH = 3584
HALF = 512
ROWS = 16
TOP = 8
CAP = 5
WIDTHS = (1024, 1280, 1280, 1280, 1280, 1024)
CHUNKS = len(WIDTHS) // 2
LOWS = tuple(sum(WIDTHS[q // CHUNKS * CHUNKS:q]) for q in range(len(WIDTHS)))
ITEMS = 2 * CHUNKS
NX = 4
NZ = 8
OFFSETS = (0, 1, -1, 2, -2, 3, -3, 4)


RING = ((None, 0, 0, 1, 2, 3, 4, 5), (None, 0, 0, 1, 2, 3, 4, 6))
TREE = (None, 0, 0, 0, 0, 3, 4, 3)
FAR = (None, None, None, None, None, 3, 4, 3)

UNITS = ((0, 16, 0), (16, 32, 0), (32, 48, 0), (32, 48, 8))

ORDER = (
    ("forward", ((0, 3),)),
    ("first", ((3,),)),
    ("plan", ((1,),)),
    ("first", ((5,), (4,),)),
    ("forward", ((0, 4),)),
    ("weigh", ((1,),)),
    ("forward", ((0, 1), (1, 4), (0, 2),)),
    ("plan", ((0,),)),
    ("first", ((0,),)),
    ("forward", ((3, 2), (0, 5),)),
    ("select", ((0, 0),)),
    ("forward", ((1, 3), (1, 1),)),
    ("first", ((1,),)),
    ("forward", ((1, 2),)),
    ("select", ((1, 0),)),
    ("first", ((2,),)),
    ("forward", ((0, 7), (0, 6),)),
    ("select", ((0, 2),)),
    ("forward", ((1, 6), (4, 2),)),
    ("select", ((0, 1),)),
    ("forward", ((5, 2), (5, 1),)),
    ("weigh", ((0,),)),
    ("exchange", ((0, 0),)),
    ("forward", ((3, 1), (1, 5),)),
    ("select", ((1, 1),)),
    ("forward", ((2, 2), (3, 4), (4, 1), (1, 7),)),
    ("select", ((1, 2),)),
    ("forward", ((2, 4), (2, 3), (2, 1),)),
    ("select", ((2, 0),)),
    ("forward", ((4, 4),)),
    ("exchange", ((0, 2),)),
    ("forward", ((3, 3),)),
    ("select", ((3, 0),)),
    ("forward", ((5, 3),)),
    ("exchange", ((0, 1),)),
    ("forward", ((3, 6), (4, 3), (2, 6), (5, 4), (2, 5),)),
    ("select", ((2, 1),)),
    ("forward", ((2, 7),)),
    ("select", ((2, 2),)),
    ("exchange", ((2, 0), (1, 2),)),
    ("select", ((5, 0),)),
    ("exchange", ((1, 1),)),
    ("gate_up", ((0, 0), (0, 1),)),
    ("forward", ((3, 5),)),
    ("exchange", ((1, 0),)),
    ("forward", ((3, 7),)),
    ("select", ((3, 2), (3, 1),)),
    ("exchange", ((3, 0),)),
    ("forward", ((5, 6), (4, 6), (4, 5),)),
    ("exchange", ((2, 1), (2, 2),)),
    ("select", ((4, 0),)),
    ("gate_up", ((1, 0), (1, 1),)),
    ("select", ((4, 1),)),
    ("gate_up", ((2, 0), (2, 1),)),
    ("activate", ((0,),)),
    ("down", ((2, 0),)),
    ("exchange", ((5, 0),)),
    ("forward", ((5, 5), (4, 7),)),
    ("select", ((4, 2),)),
    ("forward", ((5, 7),)),
    ("select", ((5, 2),)),
    ("down", ((1, 0),)),
    ("exchange", ((3, 1),)),
    ("select", ((5, 1),)),
    ("down", ((0, 0),)),
    ("send_back", ((2, 2), (2, 1),)),
    ("exchange", ((3, 2), (4, 1),)),
    ("send_back", ((1, 2), (0, 2),)),
    ("exchange", ((4, 0), (5, 2),)),
    ("send_back", ((1, 1),)),
    ("exchange", ((4, 2),)),
    ("gate_up", ((3, 0),)),
    ("exchange", ((5, 1),)),
    ("gate_up", ((3, 1),)),
    ("send_back", ((0, 1),)),
    ("gate_up", ((4, 0),)),
    ("send_back", ((1, 0),)),
    ("gate_up", ((4, 1),)),
    ("mix", ((2, 2),)),
    ("gate_up", ((5, 0), (5, 1),)),
    ("activate", ((1,),)),
    ("down", ((3, 0),)),
    ("reduce", ((2, 7),)),
    ("mix", ((0, 2),)),
    ("send_back", ((2, 0),)),
    ("mix", ((2, 1),)),
    ("reduce", ((2, 6),)),
    ("mix", ((1, 2),)),
    ("down", ((5, 0),)),
    ("reduce", ((0, 7),)),
    ("down", ((4, 0),)),
    ("mix", ((1, 1),)),
    ("reduce", ((1, 7), (1, 5),)),
    ("send_back", ((3, 2),)),
    ("mix", ((0, 1),)),
    ("send_back", ((3, 1),)),
    ("reduce", ((2, 5), (2, 4), (0, 6),)),
    ("send_back", ((4, 2), (0, 0), (5, 2), (4, 1),)),
    ("reduce", ((1, 6), (0, 5),)),
    ("mix", ((1, 0),)),
    ("reduce", ((1, 3),)),
    ("mix", ((2, 0),)),
    ("send_back", ((5, 1),)),
    ("mix", ((3, 2),)),
    ("reduce", ((3, 7), (2, 3),)),
    ("send_back", ((3, 0),)),
    ("mix", ((3, 1),)),
    ("reduce", ((3, 5), (0, 4),)),
    ("mix", ((4, 2),)),
    ("reduce", ((4, 7),)),
    ("send_back", ((4, 0),)),
    ("reduce", ((1, 4),)),
    ("send_back", ((5, 0),)),
    ("reduce", ((1, 1),)),
    ("mix", ((0, 0),)),
    ("reduce", ((0, 3), (3, 6),)),
    ("mix", ((5, 2),)),
    ("reduce", ((5, 7), (2, 2),)),
    ("mix", ((4, 1),)),
    ("reduce", ((4, 6), (4, 5), (1, 2), (2, 1), (0, 2),)),
    ("mix", ((5, 1),)),
    ("reduce", ((5, 5), (5, 6),)),
    ("mix", ((3, 0),)),
    ("reduce", ((3, 3), (3, 4), (0, 1), (4, 4),)),
    ("mix", ((4, 0),)),
    ("reduce", ((4, 3), (4, 1), (4, 2),)),
    ("mix", ((5, 0),)),
    ("reduce", ((5, 4), (5, 1), (5, 3), (3, 1),)),
    ("finish", ((1,),)),
    ("reduce", ((5, 2), (3, 2),)),
    ("finish", ((4,), (2,), (0,), (5,), (3,),)),
)
DIRECT_OUT = (0, 1, 2)
DIRECT_BACK = (5, 4)
FROM_FAR = (0, 1)


def stream(q):
    return q // CHUNKS


def width(q):
    return WIDTHS[q]


def cols(q, part=0, parts=1):
    size = width(q) // parts
    return pl.ds(LOWS[q] + part * size, size)


def half(q):
    return pl.ds(LOWS[q] // 2, width(q) // 2)


def out_parents(q):
    if q in FROM_FAR:
        return FAR
    return TREE if q in DIRECT_OUT else RING[q % 2]


def back_parents(q):
    return TREE if q in DIRECT_BACK else RING[q % 2]


def below(parents, slot):
    return [i for i in range(NZ) if parents[i] == slot]


def tiles(width, step, body):
    @pl.loop(0, width // step)
    def _(j):
        body(pl.multiple_of(j * step, step))


def dot(a, b):
    return jnp.dot(a, b, preferred_element_type=F32)


def kernel(
    tok_a, tok_b, ids_a, ids_b, gates_a, gates_b, gate_hbm, up_hbm, down_hbm,
    out_a, out_b,
    wgu, wdn, state, near, meta, table, sel, mixw, xg, snd, sndl, xs, fold, acc, hid, yo, yx, yr,
    ret, retl, rb, rbl, ct, rss, rsr,
    w_sem, y_s, y_r, yn_s, yn_r, m_s, m_r, ag_s, ag_r, x_s, x_r, ex_s, ex_r, yx_s, yx_r, rt_s, rt_r, rs_s, rs_r,
):
    section = lax.axis_index("section")
    place = lax.axis_index("expert")
    z_at, x_at = place // NX, place % NX
    partner = (section + 1 - 2 * (section % 2), place)

    def along_y(layers):
        return ((section + 2 * layers + 8) % 8, place)

    def along_z(steps):
        return (section, ((z_at + steps + 2 * NZ) % NZ) * NX + x_at)

    def along_x(steps):
        return (section, z_at * NX + (x_at + steps + NX) % NX)

    tokens = (tok_a, tok_b)
    outs = (out_a, out_b)
    sent = []
    loaded = set()
    arrived = set()
    arrived_meta = []

    def remote(src, dst, send, recv, device):
        return pltpu.make_async_remote_copy(
            src_ref=src, dst_ref=dst, send_sem=send, recv_sem=recv, device_id=device, device_id_type=MESH
        )

    def start(copy):
        copy.start()
        sent.append(copy)

    def y_copy(s):
        return remote(tokens[s].at[0], state.at[s], y_s.at[s], y_r.at[s], along_y(1 if s == 0 else -1))

    def ahead(q):
        return 1 if stream(q) == 0 else -1

    def yn_copy(q):
        return remote(
            near.at[stream(q), :, cols(q)], xg.at[stream(q), pl.ds(0, ROWS), cols(q)],
            yn_s.at[q], yn_r.at[q], along_y(ahead(q)),
        )

    def meta_copy(i):
        return remote(
            meta.at[pl.ds(0, ROWS)], meta.at[pl.ds(ROWS * i, ROWS)], m_s.at[i], m_r.at[i], along_z(OFFSETS[i])
        )

    def ag_copy(q, i):
        p, to = out_parents(q)[i], xg.at[stream(q), pl.ds(ROWS * i, ROWS), cols(q)]
        if p is None:
            device = (along_y(ahead(q))[0], along_z(OFFSETS[i])[1])
            return remote(near.at[stream(q), :, cols(q)], to, ag_s.at[q, i], ag_r.at[q, i], device)
        return remote(
            xg.at[stream(q), pl.ds(ROWS * p, ROWS), cols(q)], to,
            ag_s.at[q, i], ag_r.at[q, i], along_z(OFFSETS[i] - OFFSETS[p]),
        )

    def x_copy(q, u, dx):
        sems = (x_s.at[q, u, dx], x_r.at[q, u, dx], along_x(dx))
        rows, s = pl.ds(16 * dx, 16), stream(q)
        if u == 2:
            return remote(sndl.at[s, rows, half(q)], fold.at[s, 0, rows, half(q)], *sems)
        return remote(snd.at[s, u, rows, cols(q)], xs.at[s, pl.ds(64 * u + 16 * dx, 16), cols(q)], *sems)

    def ex_copy(q, u):
        sems, s = (ex_s.at[q, u], ex_r.at[q, u], partner), stream(q)
        if u == 2:
            return remote(fold.at[s, 0, :, half(q)], fold.at[s, 1, :, half(q)], *sems)
        return remote(xs.at[s, pl.ds(64 * u, 64), cols(q)], xs.at[s, pl.ds(128 + 64 * u, 64), cols(q)], *sems)

    def yx_copy(q):
        s = stream(q)
        return remote(yx.at[s, :, cols(q)], yr.at[s, :, cols(q)], yx_s.at[q], yx_r.at[q], partner)

    def rt_copy(q, u, dx):
        sems = (rt_s.at[q, u, dx], rt_r.at[q, u, dx], along_x(-dx))
        rows, s = pl.ds(16 * dx, 16), stream(q)
        if u == 2:
            return remote(retl.at[s, rows, half(q)], rbl.at[s, rows, half(q)], *sems)
        return remote(ret.at[s, u, rows, cols(q)], rb.at[s, u, rows, cols(q)], *sems)

    def rs_copy(q, i):
        p, s = back_parents(q)[i], stream(q)
        rows = pl.ds(ROWS * i, ROWS)
        return remote(
            rss.at[s, rows, cols(q)], rsr.at[s, rows, cols(q)],
            rs_s.at[q, i], rs_r.at[q, i], along_z(OFFSETS[p] - OFFSETS[i]),
        )

    loads = [
        pltpu.make_async_copy(gate_hbm.at[0, 0], wgu.at[:, pl.ds(0, HALF)], w_sem.at[0]),
        pltpu.make_async_copy(up_hbm.at[0, 0], wgu.at[:, pl.ds(HALF, HALF)], w_sem.at[1]),
        pltpu.make_async_copy(down_hbm.at[0, 0], wdn, w_sem.at[2]),
    ]
    for load in loads:
        load.start()

    barrier = pltpu.get_barrier_semaphore()
    friends = [along_y(1), along_y(-1), partner]
    if FROM_FAR:
        friends += [(along_y(y)[0], along_z(OFFSETS[i])[1]) for y in (1, -1) for i in range(1, 5)]
    friends += [along_z(OFFSETS[i]) for i in range(1, NZ)]
    friends += [along_x(dx) for dx in range(1, NX)]
    for friend in friends:
        pl.semaphore_signal(barrier, inc=1, device_id=friend, device_id_type=MESH)

    lane8 = lax.broadcasted_iota(jnp.int32, (TOP, 128), 1)
    row8 = lax.broadcasted_iota(jnp.int32, (TOP, 128), 0)
    block = jnp.zeros((ROWS, 128), F32)
    for s, (ids_ref, gates_ref) in enumerate(((ids_a, gates_a), (ids_b, gates_b))):
        ids = ids_ref[0, section].astype(F32).astype(BF16)
        gates = gates_ref[0, section]
        high = gates.astype(BF16)
        low = (gates - high.astype(F32)).astype(BF16)
        for j, part in enumerate((ids, high, low)):
            spot = jnp.where(lane8 == row8 + (24 * s + 8 * j), 1.0, 0.0).astype(BF16)
            block = block + lax.dot_general(part, spot, (((0,), (0,)), ((), ())), preferred_element_type=F32)
    meta[0:ROWS, :] = block.astype(BF16)

    def norm(s):
        values = tokens[s][0].astype(F32)
        scale = lax.rsqrt(jnp.mean(values * values, axis=-1, keepdims=True) + 1e-06)
        near[s] = (values * scale).astype(BF16)

    def first(q):
        yn_copy(q).wait_recv()
        z_send(q, 0)

    def z_send(q, slot):
        for i in below(out_parents(q), slot):
            start(ag_copy(q, i))

    def forward(q, slot):
        ag_copy(q, slot).wait_recv()
        z_send(q, slot)

    def spots(s):
        if not arrived_meta:
            arrived_meta.append(True)
            for i in range(1, NZ):
                meta_copy(i).wait_recv()
            table[...] = meta[...].astype(F32).T
        ids_t, high_t, low_t = (table[24 * s + 8 * j:24 * s + 8 * j + 8] for j in range(3))
        named, highs, lows = [], [], []
        for dx in range(NX):
            expert_at = (z_at * NX + (x_at + dx) % NX).astype(F32)
            same = jnp.where(ids_t == expert_at, 1.0, 0.0)
            named.append(jnp.sum(same, axis=0, keepdims=True))
            highs.append(jnp.sum(same * high_t, axis=0, keepdims=True))
            lows.append(jnp.sum(same * low_t, axis=0, keepdims=True))
        stacked = jnp.concatenate(named + [jnp.zeros((8 - NX, 128), F32)], axis=0)
        lane = lax.broadcasted_iota(jnp.int32, (128, 128), 1)
        row = lax.broadcasted_iota(jnp.int32, (128, 128), 0)
        earlier = jnp.where((row // ROWS == lane // ROWS) & (row < lane), 1.0, 0.0).astype(BF16)
        before = dot(stacked.astype(BF16), earlier).astype(jnp.int32)
        first = (lax.broadcasted_iota(jnp.int32, (1, 128), 1) // ROWS) * CAP
        rows = [jnp.where(named[dx] > 0.5, first + before[dx:dx + 1], -1) for dx in range(NX)]
        return rows, highs, lows

    def hits(spot, u, dx, count):
        least, most, shift = UNITS[u]
        target = jnp.where((spot >= least) & (spot < most), spot - least + shift + 16 * dx, -1)
        return lax.broadcasted_iota(jnp.int32, (count, 128), 0) == target

    def plan(s):
        rows, _, _ = spots(s)
        for u in range(4):
            picks = jnp.zeros((64, 128), F32)
            for dx in range(NX):
                picks = jnp.where(hits(rows[dx], u, dx, 64), 1.0, picks)
            sel[s, u] = picks.astype(BF16)

    def weigh(s):
        rows, highs, lows = spots(s)
        for u in range(4):
            high_w = jnp.zeros((128, 128), F32)
            low_w = jnp.zeros((128, 128), F32)
            for dx in range(NX):
                hit = hits(rows[dx], u, dx, 128)
                high_w = jnp.where(hit, highs[dx], high_w)
                low_w = jnp.where(hit, lows[dx], low_w)
            mixw[s, u, 0] = high_w.T.astype(BF16)
            mixw[s, u, 1] = low_w.T.astype(BF16)

    def select(q, u):
        s = stream(q)
        if u == 2:
            value = dot(sel[s, 2], xg[s, :, cols(q, 0, 2)]) + dot(sel[s, 3], xg[s, :, cols(q, 1, 2)])
            value = value.astype(BF16)
            fold[s, 0, 0:16, half(q)] = value[0:16]
            sndl[s, 16:64, half(q)] = value[16:64]
        else:
            depth = 64 if u == 0 else 112
            value = dot(sel[s, u][:, 0:depth], xg[s, 0:depth, cols(q)]).astype(BF16)
            xs[s, 64 * u:64 * u + 16, cols(q)] = value[0:16]
            snd[s, u, 16:64, cols(q)] = value[16:64]
        for dx in (2, 1, 3):
            start(x_copy(q, u, dx))

    def exchange(q, u):
        for dx in (1, 3, 2):
            x_copy(q, u, dx).wait_recv()
        start(ex_copy(q, u))

    def gate_up(q, part):
        s, c = stream(q), q % CHUNKS
        if part == 0:
            unfold(q)
        wait_load(part)
        side = pl.ds(part * HALF, HALF)
        value = dot(xs[s, :, cols(q)], wgu[cols(q), side])
        acc[:, side] = value if c == 0 else acc[:, side] + value

    def unfold(q):
        s = stream(q)
        for u in range(3):
            ex_copy(q, u).wait_recv()
        for h in range(2):
            part = fold[s, h, :, half(q)].astype(F32)
            left = jnp.concatenate([part[16 * dx:16 * dx + 8] for dx in range(NX)], axis=0)
            right = jnp.concatenate([part[16 * dx + 8:16 * dx + 16] for dx in range(NX)], axis=0)
            xs[s, 256 + 32 * h:288 + 32 * h, cols(q, 0, 2)] = left.astype(BF16)
            xs[s, 256 + 32 * h:288 + 32 * h, cols(q, 1, 2)] = right.astype(BF16)

    def activate(s):
        def body(at):
            gate = acc[:, pl.ds(at, 128)]
            up = acc[:, pl.ds(HALF + at, 128)]
            hid[s, :, pl.ds(at, 128)] = (gate / (1.0 + jnp.exp(-gate)) * up).astype(BF16)
        tiles(HALF, 128, body)

    def down(q, part):
        s = stream(q)
        wait_load(2)
        for j in range(width(q) // 256):
            at = pl.ds(LOWS[q] + 256 * j, 256)
            value = dot(hid[s], wdn[:, at])
            yo[s, 0:128, at] = value[0:128]
            yo[s, 128:160, at] = value[256:288]
            yx[s, 0:128, at] = value[128:256].astype(BF16)
            yx[s, 128:160, at] = value[288:320].astype(BF16)
        start(yx_copy(q))

    def send_back(q, u):
        s = stream(q)
        if u == 2:
            yx_copy(q).wait_recv()
            rows = pl.ds(128, 32)
            near_half, far_half = (
                yo[s, rows, cols(q, k, 2)] + yr[s, rows, cols(q, k, 2)].astype(F32) for k in range(2)
            )
            for dx in range(NX):
                part = slice(8 * dx, 8 * dx + 8)
                both = jnp.concatenate([near_half[part], far_half[part]], axis=0).astype(BF16)
                (rbl if dx == 0 else retl)[s, 16 * dx:16 * dx + 16, half(q)] = both
        else:
            rows = pl.ds(64 * u, 64)
            both = (yo[s, rows, cols(q)] + yr[s, rows, cols(q)].astype(F32)).astype(BF16)
            rb[s, u, 0:16, cols(q)] = both[0:16]
            ret[s, u, 16:64, cols(q)] = both[16:64]
        for dx in (2, 1, 3):
            start(rt_copy(q, u, dx))

    def mix(q, u):
        s = stream(q)
        for dx in (1, 3, 2):
            rt_copy(q, u, dx).wait_recv()

        def weights(k, low, high):
            return jnp.concatenate(
                [mixw[s, k, 0, low:high][:, 0:64], mixw[s, k, 1, low:high][:, 0:64]], axis=0
            )

        if u == 2:
            for k in range(2):
                value = dot(weights(2 + k, 96, 128), rbl[s, :, half(q)])
                ct[s, 96:128, cols(q, k, 2)] = value[0:32] + value[32:64]
        else:
            low, high, shared = (48, 112, 96) if u == 1 else (0, 64, 48)
            for k in range(2):
                at = cols(q, k, 2)
                both = dot(weights(u, low, high), rb[s, u, :, at])
                value = both[0:64] + both[64:128]
                ct[s, low:shared, at] = value[0:shared - low]
                ct[s, shared:high, at] = ct[s, shared:high, at] + value[shared - low:]

    def gathered(q, slot):
        s = stream(q)
        total = ct[s, ROWS * slot:ROWS * (slot + 1), cols(q)]
        for i in below(back_parents(q), slot):
            rs_copy(q, i).wait_recv()
            total = total + rsr[s, ROWS * i:ROWS * (i + 1), cols(q)].astype(F32)
        return total

    def reduce(q, slot):
        rss[stream(q), ROWS * slot:ROWS * (slot + 1), cols(q)] = gathered(q, slot).astype(BF16)
        start(rs_copy(q, slot))

    def finish(q):
        s = stream(q)
        if s not in arrived:
            y_copy(s).wait_recv()
            arrived.add(s)
        total = gathered(q, 0) + state[s, :, cols(q)].astype(F32)
        outs[s][0, :, cols(q)] = total.astype(BF16)

    def wait_load(i):
        if i not in loaded:
            loads[i].wait()
            loaded.add(i)

    norm(0)
    norm(1)
    pl.semaphore_wait(barrier, len(friends))
    for q in range(ITEMS):
        for i in (3, 4, 1, 2):
            if q in FROM_FAR:
                start(ag_copy(q, i))
        start(yn_copy(q))
        if q == 0:
            for i in range(1, NZ):
                start(meta_copy(i))
    for s in range(2):
        start(y_copy(s))
    known = dict(
        first=first, plan=plan, weigh=weigh, forward=forward, select=select, exchange=exchange, gate_up=gate_up,
        activate=activate, down=down, send_back=send_back, mix=mix, reduce=reduce, finish=finish,
    )
    steps = [functools.partial(known[name], *which) for name, turns in ORDER for which in turns]
    for step in steps:
        step()
    for copy in sent:
        copy.wait_send()


def hand_over(a_ref, b_ref, out_a, out_b):
    out_a[...] = a_ref[...]
    out_b[...] = b_ref[...]


def layer(*args):
    vmem = pl.BlockSpec(memory_space=pltpu.VMEM)
    hbm = pl.BlockSpec(memory_space=pl.ANY)
    dma = pltpu.SemaphoreType.DMA
    q = ITEMS
    state = jax.ShapeDtypeStruct((1, ROWS, WIDTH), BF16)
    return pl.pallas_call(
        kernel,
        out_shape=(state, state),
        in_specs=[vmem] * 6 + [hbm] * 3,
        out_specs=(vmem, vmem),
        scratch_shapes=[
            pltpu.VMEM((WIDTH, 2 * HALF), BF16),
            pltpu.VMEM((HALF, WIDTH), BF16),
            pltpu.VMEM((2, ROWS, WIDTH), BF16),
            pltpu.VMEM((2, ROWS, WIDTH), BF16),
            pltpu.VMEM((128, 128), BF16),
            pltpu.VMEM((128, 128), F32),
            pltpu.VMEM((2, 4, 64, 128), BF16),
            pltpu.VMEM((2, 4, 2, 128, 128), BF16),
            pltpu.VMEM((2, 128, WIDTH), BF16),
            pltpu.VMEM((2, 2, 64, WIDTH), BF16),
            pltpu.VMEM((2, 64, WIDTH // 2), BF16),
            pltpu.VMEM((2, 320, WIDTH), BF16),
            pltpu.VMEM((2, 2, 64, WIDTH // 2), BF16),
            pltpu.VMEM((320, 2 * HALF), F32),
            pltpu.VMEM((2, 320, HALF), BF16),
            pltpu.VMEM((2, 160, WIDTH), F32),
            pltpu.VMEM((2, 160, WIDTH), BF16),
            pltpu.VMEM((2, 160, WIDTH), BF16),
            pltpu.VMEM((2, 2, 64, WIDTH), BF16),
            pltpu.VMEM((2, 64, WIDTH // 2), BF16),
            pltpu.VMEM((2, 2, 64, WIDTH), BF16),
            pltpu.VMEM((2, 64, WIDTH // 2), BF16),
            pltpu.VMEM((2, 128, WIDTH), F32),
            pltpu.VMEM((2, 128, WIDTH), BF16),
            pltpu.VMEM((2, 128, WIDTH), BF16),
            dma((3,)),
            dma((2,)), dma((2,)),
            dma((q,)), dma((q,)),
            dma((NZ,)), dma((NZ,)),
            dma((q, NZ)), dma((q, NZ)),
            dma((q, 3, NX)), dma((q, 3, NX)),
            dma((q, 3)), dma((q, 3)),
            dma((q,)), dma((q,)),
            dma((q, 3, NX)), dma((q, 3, NX)),
            dma((q, NZ)), dma((q, NZ)),
        ],
        compiler_params=pltpu.CompilerParams(
            collective_id=0, has_side_effects=True, vmem_limit_bytes=60 * 2**20
        ),
        name="routed_layer",
    )(*args)


def body(tok_a, tok_b, ids_a, ids_b, gates_a, gates_b, gate_proj, up_proj, down_proj):
    small = [jnp.transpose(v, (0, 1, 3, 2)) for v in (ids_a, ids_b, gates_a, gates_b)]
    done = layer(tok_a, tok_b, *small, gate_proj, up_proj, down_proj)
    return pl.pallas_call(
        hand_over,
        out_shape=tuple(jax.ShapeDtypeStruct(v.shape, v.dtype) for v in done),
        name="hand_over",
    )(*done)


def solution(mesh):
    states = P("section", "expert", None)
    routes = P(None, None, "expert", None)
    weights = P("section", "expert", None, None)
    return jax.shard_map(
        body,
        mesh=mesh,
        in_specs=(states, states, routes, routes, routes, routes, weights, weights, weights),
        out_specs=(states, states),
        check_vma=False,
    )
```

time: 97.5 us -> 87 us (0.89)
  Pallas kernels: 95.7 us -> 84.7 us
    pallas_call x1, Pallas kernels: 8.07 us -> 1.65 us  [body(): pl.pallas_call(hand_over, out_shape=tuple((jax.ShapeDtypeStruct(v.shape,...]
    pallas_call x1, Pallas kernels: 87.7 us -> 83.1 us  [layer(): pl.pallas_call(kernel, out_shape=(state, state), in_specs=[vmem] * 6 + [h...]
where the time goes in v3:
time: 87 us; the launch traced here: 85.3 us
  Pallas kernels  84.7 us (97%)
    pallas_call x1, Pallas kernels, layer(): pl.pallas_call(kernel, out_shape=(state, state), in_specs=[vmem] * 6 + [h...  83.1 us

profile of v3, /device:TPU:4, one launch (start us, length us, event | category | flops | bytes accessed | tf_op | source)
XLA Modules:
  0.0 85.3 jit_solution(5543451507203731496)
XLA Ops:
  0.6 83.1 %routed_layer.1 = (bf16[1,16,3584]{2,1,0:T(8,128)(2,1)}, bf16[1,16,3584]{2,1,0:T(8,128)(2,1)}) custom-call(bf16[1,16,3584]{2,1,0:T(8,128)(2,1)} %tok_a.1, bf16[1,16,3584]{2,1,0:T(8,128)(2,1)} %tok_b.1, s32[1,8,8,16]{3,2,1,0:T(8,128)} %bitcast.4, s32[1,8,8,16]{3,2,1,0:T(8,128)} %bitcast.5, f32[1,8,8,16]{3,2,1,0:T(8,128)} %bitcast.6, f32[1,8,8,16]{3,2,1,0:T(8,128)} %bitcast.7, ...), custom_call_target="tpu_custom_call" | custom-call | tf_op jit(solution)/shard_map/routed_layer/pallas_call | solution.py:566
  83.7 1.6 %hand_over.1 = (bf16[1,16,3584]{2,1,0:T(8,128)(2,1)}, bf16[1,16,3584]{2,1,0:T(8,128)(2,1)}) custom-call(bf16[1,16,3584]{2,1,0:T(8,128)(2,1)} %get-tuple-element.4.a_ref, bf16[1,16,3584]{2,1,0:T(8,128)(2,1)} %get-tuple-element.5.b_ref), custom_call_target="tpu_custom_call" | custom-call | tf_op jit(solution)/shard_map/hand_over/pallas_call | solution.py:618

commit v4 on v3

--- a/solution.py
+++ b/solution.py
@@ -213,9 +213,9 @@
 def kernel(
     tok_a, tok_b, ids_a, ids_b, gates_a, gates_b, gate_hbm, up_hbm, down_hbm,
     out_a, out_b,
-    wgu, wdn, state, near, meta, table, sel, mixw, xg, snd, sndl, xs, fold, acc, hid, yo, yx, yr,
+    ended, wgu, wdn, state, near, meta, table, sel, mixw, xg, snd, sndl, xs, fold, acc, hid, yo, yx, yr,
     ret, retl, rb, rbl, ct, rss, rsr,
-    w_sem, y_s, y_r, yn_s, yn_r, m_s, m_r, ag_s, ag_r, x_s, x_r, ex_s, ex_r, yx_s, yx_r, rt_s, rt_r, rs_s, rs_r,
+    out_sem, w_sem, y_s, y_r, yn_s, yn_r, m_s, m_r, ag_s, ag_r, x_s, x_r, ex_s, ex_r, yx_s, yx_r, rt_s, rt_r, rs_s, rs_r,
 ):
     section = lax.axis_index("section")
     place = lax.axis_index("expert")
@@ -236,6 +236,7 @@
     sent = []
     loaded = set()
     arrived = set()
+    writes = []
     arrived_meta = []
 
     def remote(src, dst, send, recv, device):
@@ -521,7 +522,10 @@
             y_copy(s).wait_recv()
             arrived.add(s)
         total = gathered(q, 0) + state[s, :, cols(q)].astype(F32)
-        outs[s][0, :, cols(q)] = total.astype(BF16)
+        ended[s, :, cols(q)] = total.astype(BF16)
+        write = pltpu.make_async_copy(ended.at[s, :, cols(q)], outs[s].at[0, :, cols(q)], out_sem.at[q])
+        write.start()
+        writes.append(write)
 
     def wait_load(i):
         if i not in loaded:
@@ -550,6 +554,8 @@
         step()
     for copy in sent:
         copy.wait_send()
+    for write in writes:
+        write.wait()
 
 
 def hand_over(a_ref, b_ref, out_a, out_b):
@@ -567,8 +573,9 @@
         kernel,
         out_shape=(state, state),
         in_specs=[vmem] * 6 + [hbm] * 3,
-        out_specs=(vmem, vmem),
+        out_specs=(hbm, hbm),
         scratch_shapes=[
+            pltpu.VMEM((2, ROWS, WIDTH), BF16),
             pltpu.VMEM((WIDTH, 2 * HALF), BF16),
             pltpu.VMEM((HALF, WIDTH), BF16),
             pltpu.VMEM((2, ROWS, WIDTH), BF16),
@@ -594,6 +601,7 @@
             pltpu.VMEM((2, 128, WIDTH), F32),
             pltpu.VMEM((2, 128, WIDTH), BF16),
             pltpu.VMEM((2, 128, WIDTH), BF16),
+            dma((q,)),
             dma((3,)),
             dma((2,)), dma((2,)),
             dma((q,)), dma((q,)),

time: 87 us -> 86.6 us (level)
  no operation moved by 1% of the time
where the time goes in v4:
time: 86.6 us; the launch traced here: 85 us
  Pallas kernels  84.3 us (97%)
    pallas_call x1, Pallas kernels, layer(): pl.pallas_call(kernel, out_shape=(state, state), in_specs=[vmem] * 6 + [h...  82.7 us

profile of v4, /device:TPU:4, one launch (start us, length us, event | category | flops | bytes accessed | tf_op | source)
XLA Modules:
  0.0 85.0 jit_solution(1498306857667664751)
XLA Ops:
  0.6 82.7 %routed_layer.1 = (bf16[1,16,3584]{2,1,0:T(8,128)(2,1)}, bf16[1,16,3584]{2,1,0:T(8,128)(2,1)}) custom-call(bf16[1,16,3584]{2,1,0:T(8,128)(2,1)} %tok_a.1, bf16[1,16,3584]{2,1,0:T(8,128)(2,1)} %tok_b.1, s32[1,8,8,16]{3,2,1,0:T(8,128)} %bitcast.4, s32[1,8,8,16]{3,2,1,0:T(8,128)} %bitcast.5, f32[1,8,8,16]{3,2,1,0:T(8,128)} %bitcast.6, f32[1,8,8,16]{3,2,1,0:T(8,128)} %bitcast.7, ...), custom_call_target="tpu_custom_call" | custom-call | tf_op jit(solution)/shard_map/routed_layer/pallas_call | solution.py:572
  83.3 1.6 %hand_over.1 = (bf16[1,16,3584]{2,1,0:T(8,128)(2,1)}, bf16[1,16,3584]{2,1,0:T(8,128)(2,1)}) custom-call(bf16[1,16,3584]{2,1,0:T(8,128)(2,1)} %get-tuple-element.4.a_ref, bf16[1,16,3584]{2,1,0:T(8,128)(2,1)} %get-tuple-element.5.b_ref), custom_call_target="tpu_custom_call" | custom-call | tf_op jit(solution)/shard_map/hand_over/pallas_call | solution.py:626
